TPU v7x, 128 devices: a whole 4x4x4 slice. The times are simulated.
128 devices in a mesh: seq: 32 (over z, x, core), tp: 4 (over y).
Axes of the slice: x: 4, y: 4, z: 4, core: 2. Of those that a mesh axis runs over, the one named last changes fastest.
Arguments:
- tokens: bfloat16 [8192, 5120], P('seq', 'tp'), may hold values from -21 to 21
- w_query: bfloat16 [5120, 2560], P(None, 'tp'), may hold values from -1.1 to 1.1
- b_query: bfloat16 [2560], P('tp'), may hold values from -3 to 3
- w_key: bfloat16 [5120, 512], P(None, 'tp'), may hold values from -1.1 to 1.1
- key_bias: bfloat16 [512], P('tp'), may hold values from -3 to 3
- value_weight: bfloat16 [5120, 512], P(None, 'tp'), may hold values from -0.078125 to 0.078125
- value_bias: bfloat16 [512], P('tp'), may hold values from -3 to 3
- w_out: bfloat16 [2560, 5120], P('tp'), may hold values from -0.5 to 0.5
- doc_lengths: int32 [4], replicated, may hold values from 1 to 4096, 8192 in all
- grad_out: bfloat16 [8192, 5120], P('seq', 'tp'), may hold values from -1.1953125 to 1.1953125
Outputs:
- output: bfloat16 [8192, 5120], P('seq', 'tp')
- grad_tokens: bfloat16 [8192, 5120], P('seq', 'tp')
All inputs are finite; a program needn't handle non-finite values.
Results may differ from a plain program's by a relative error of at most 0.025.
Values may be sent and summed in bfloat16 or wider, within the bound.
A program may use at most 128 MiB of HBM per device.

v0:
```python
import jax
import jax.numpy as jnp
from jax import lax
from jax.sharding import PartitionSpec as P

theta_base = 1000000.0
neg_large = -1e30


def from_behind(value, axis, by):
    devices = lax.axis_size(axis)
    pairs = [(i, i + by) for i in range(devices) if 0 <= i + by < devices]
    return lax.ppermute(value, axis, pairs)


def doc_bounds(doc_lengths):
    doc_ends = jnp.cumsum(doc_lengths)
    return (doc_ends - doc_lengths, doc_ends)


def start_of(token_index, doc_starts, doc_ends):
    inside = (token_index[:, None] >= doc_starts[None, :]) & (
        token_index[:, None] < doc_ends[None, :]
    )
    return jnp.sum(jnp.where(inside, doc_starts[None, :], 0), axis=1)


def rope_tables(position, head_dim):
    halfway = head_dim // 2
    frequency = theta_base ** (-2.0 * jnp.arange(halfway, dtype=jnp.float32) / head_dim)
    angles = position.astype(jnp.float32)[:, None] * frequency[None, :]
    return (jnp.cos(angles)[:, None, :], jnp.sin(angles)[:, None, :])


def apply_rotation(values, cosine_table, sine_table):
    halfway = values.shape[-1] // 2
    former = values[..., :halfway]
    latter = values[..., halfway:]
    return jnp.concatenate(
        [former * cosine_table - latter * sine_table, latter * cosine_table + former * sine_table],
        axis=-1,
    )


def inverse_rotation(values, cosine_table, sine_table):
    halfway = values.shape[-1] // 2
    former = values[..., :halfway]
    latter = values[..., halfway:]
    return jnp.concatenate(
        [former * cosine_table + latter * sine_table, latter * cosine_table - former * sine_table],
        axis=-1,
    )


def allowed_mask(row_index, row_start, col_index, col_start):
    return (col_index[None, :] <= row_index[:, None]) & (col_start[None, :] == row_start[:, None])


def passthrough(kept):
    return kept


def dot_back(left_side, weight):
    return lax.dot_general(
        left_side, weight, (((1,), (1,)), ((), ())), preferred_element_type=jnp.float32
    )


def score_terms(query_part, grad_part, lse_part, delta_part, key_mat, value_mat, allowed, factor):
    scores = (
        jnp.einsum("rgd,kd->grk", query_part, key_mat, preferred_element_type=jnp.float32) * factor
    )
    prob = jnp.where(allowed[None], jnp.exp(scores - lse_part[:, :, None]), 0.0)
    dprob = jnp.einsum("rgd,kd->grk", grad_part, value_mat, preferred_element_type=jnp.float32)
    dscore = prob * (dprob - delta_part[:, :, None])
    return (prob.astype(jnp.bfloat16), dscore.astype(jnp.bfloat16))


def attend(query_matrix, query_index, query_start, all_pairs, doc_starts, doc_ends, key_span):
    row_count, query_groups, head_dim = query_matrix.shape
    factor = head_dim ** (-0.5)
    highest = jnp.max(query_index)
    lowest = jnp.min(query_start)

    def attend_one_span(totals, step_id):
        begin_row = step_id * key_span

        def attend_active(totals):
            best_score, mass_sum, accum_out = totals
            portion = lax.dynamic_slice_in_dim(all_pairs, begin_row, key_span, 0)
            key_index = begin_row + jnp.arange(key_span, dtype=jnp.int32)
            allowed = allowed_mask(
                query_index, query_start, key_index, start_of(key_index, doc_starts, doc_ends)
            )[None]
            scores = (
                jnp.einsum(
                    "rgd,kd->grk", query_matrix, portion[:, 0], preferred_element_type=jnp.float32
                )
                * factor
            )
            new_best = jnp.maximum(
                best_score, jnp.max(jnp.where(allowed, scores, neg_large), axis=2)
            )
            weights = jnp.where(allowed, jnp.exp(scores - new_best[:, :, None]), 0.0)
            shrink = jnp.exp(best_score - new_best)
            mass_sum = mass_sum * shrink + jnp.sum(weights, axis=2)
            summed = jnp.einsum(
                "grk,kd->grd",
                weights.astype(jnp.bfloat16),
                portion[:, 1],
                preferred_element_type=jnp.float32,
            )
            accum_out = accum_out * shrink[:, :, None] + summed
            return (new_best, mass_sum, accum_out)

        is_live = (begin_row <= highest) & (begin_row + key_span > lowest)
        return (lax.cond(is_live, attend_active, passthrough, totals), None)

    start_state = (
        jnp.full((query_groups, row_count), neg_large, jnp.float32),
        jnp.zeros((query_groups, row_count), jnp.float32),
        jnp.zeros((query_groups, row_count, head_dim), jnp.float32),
    )
    final_state, unused = lax.scan(
        attend_one_span, start_state, jnp.arange(all_pairs.shape[0] // key_span)
    )
    best_score, mass_sum, accum_out = final_state
    attended_output = jnp.transpose(accum_out / mass_sum[:, :, None], (1, 0, 2)).astype(
        jnp.bfloat16
    )
    return (attended_output, best_score + jnp.log(mass_sum))


def query_grads(
    query_rows,
    grad_rows,
    log_mass,
    delta_cols,
    query_index,
    query_start,
    all_pairs,
    doc_starts,
    doc_ends,
    key_span,
):
    row_count, query_groups, head_dim = query_rows.shape
    factor = head_dim ** (-0.5)
    highest = jnp.max(query_index)
    lowest = jnp.min(query_start)
    key_total = all_pairs.shape[0]

    def query_one_span(totals, step_id):
        begin_row = step_id * key_span

        def query_active(totals):
            grad_query, running_terms = totals
            portion = lax.dynamic_slice_in_dim(all_pairs, begin_row, key_span, 0)
            key_index = begin_row + jnp.arange(key_span, dtype=jnp.int32)
            allowed = allowed_mask(
                query_index, query_start, key_index, start_of(key_index, doc_starts, doc_ends)
            )
            prob_b, dscore_b = score_terms(
                query_rows,
                grad_rows,
                log_mass,
                delta_cols,
                portion[:, 0],
                portion[:, 1],
                allowed,
                factor,
            )
            grad_query = (
                grad_query
                + jnp.einsum(
                    "grk,kd->rgd", dscore_b, portion[:, 0], preferred_element_type=jnp.float32
                )
                * factor
            )
            return (grad_query, running_terms)

        is_live = (begin_row <= highest) & (begin_row + key_span > lowest)
        return (lax.cond(is_live, query_active, passthrough, totals), None)

    start_terms = jnp.zeros((1, 2, head_dim), jnp.float32)
    start_state = (jnp.zeros((row_count, query_groups, head_dim), jnp.float32), start_terms)
    final_state, unused = lax.scan(query_one_span, start_state, jnp.arange(key_total // key_span))
    return final_state


def local(
    tokens,
    w_query,
    b_query,
    w_key,
    key_bias,
    value_weight,
    value_bias,
    w_out,
    doc_lengths,
    grad_out,
):
    shards = lax.axis_size("seq")
    shard_id = lax.axis_index("seq")
    local_rows = tokens.shape[0]
    head_dim = w_key.shape[1]
    query_groups = w_query.shape[1] // head_dim
    key_span = 512
    factor = head_dim ** (-0.5)
    doc_starts, doc_ends = doc_bounds(doc_lengths)
    full_tokens, full_grads = (
        lax.all_gather(tokens, "tp", axis=1, tiled=True),
        lax.all_gather(grad_out, "tp", axis=1, tiled=True),
    )
    own_index = shard_id * local_rows + jnp.arange(local_rows, dtype=jnp.int32)
    own_start = start_of(own_index, doc_starts, doc_ends)
    own_cos, own_sin = rope_tables(own_index - own_start, head_dim)
    query_raw = jnp.dot(full_tokens, w_query, preferred_element_type=jnp.float32) + b_query.astype(
        jnp.float32
    )
    query_own = apply_rotation(
        query_raw.reshape(local_rows, query_groups, head_dim), own_cos, own_sin
    ).astype(jnp.bfloat16)
    key_unrotated = jnp.dot(
        full_tokens, w_key, preferred_element_type=jnp.float32
    ) + key_bias.astype(jnp.float32)
    key_own = apply_rotation(
        key_unrotated.reshape(local_rows, 1, head_dim), own_cos, own_sin
    ).astype(jnp.bfloat16)
    value_unprojected = jnp.dot(
        full_tokens, value_weight, preferred_element_type=jnp.float32
    ) + value_bias.astype(jnp.float32)
    value_own = value_unprojected.astype(jnp.bfloat16)
    own_pairs = jnp.concatenate([key_own, value_own[:, None, :]], axis=1)
    all_pairs = lax.all_gather(own_pairs, "seq", axis=0, tiled=True)
    attended_gradient = (
        dot_back(full_grads, w_out).astype(jnp.bfloat16).reshape(local_rows, query_groups, head_dim)
    )
    query_start = start_of(own_index, doc_starts, doc_ends)
    row_cos, row_sin = rope_tables(own_index - query_start, head_dim)
    attended_piece, log_piece = attend(
        query_own, own_index, query_start, all_pairs, doc_starts, doc_ends, key_span
    )
    attended_output = attended_piece.reshape(local_rows, query_groups * head_dim)
    partial_out = jnp.dot(attended_output, w_out, preferred_element_type=jnp.float32)
    output = lax.psum_scatter(
        partial_out.astype(jnp.bfloat16), "tp", scatter_dimension=1, tiled=True
    )
    delta_rows = jnp.sum(
        attended_gradient.astype(jnp.float32) * attended_piece.astype(jnp.float32), axis=2
    )
    grad_piece, unused = query_grads(
        query_own,
        attended_gradient,
        log_piece,
        delta_rows.T,
        own_index,
        query_start,
        all_pairs,
        doc_starts,
        doc_ends,
        key_span,
    )
    attended_own = attended_output.reshape(local_rows, query_groups, head_dim)
    delta_own = jnp.sum(
        attended_gradient.astype(jnp.float32) * attended_own.astype(jnp.float32), axis=2
    ).T
    key_mat = own_pairs[:, 0]
    value_mat = own_pairs[:, 1]
    own_high = shard_id * local_rows + local_rows - 1

    def absorb(totals, rows_pair, stats_pair, source_shard):
        part_query, part_grad = rows_pair
        part_lse, part_delta = stats_pair
        row_index = source_shard * local_rows + jnp.arange(local_rows, dtype=jnp.int32)
        row_start = start_of(row_index, doc_starts, doc_ends)

        def absorb_active(totals):
            allowed = allowed_mask(row_index, row_start, own_index, own_start)
            prob_b, dscore_b = score_terms(
                part_query, part_grad, part_lse, part_delta, key_mat, value_mat, allowed, factor
            )
            grad_key = (
                jnp.einsum("grk,rgd->kd", dscore_b, part_query, preferred_element_type=jnp.float32)
                * factor
            )
            grad_value = jnp.einsum(
                "grk,rgd->kd", prob_b, part_grad, preferred_element_type=jnp.float32
            )
            return totals + jnp.stack([grad_key, grad_value], axis=1)

        is_live = (source_shard < shards) & (jnp.min(row_start) <= own_high)
        return lax.cond(is_live, absorb_active, passthrough, totals)

    first_rows = (query_own, attended_gradient)
    first_stats = (log_piece, delta_own)
    start_totals = absorb(
        jnp.zeros((local_rows, 2, head_dim), jnp.float32), first_rows, first_stats, shard_id
    )

    def one_hop(step, state):
        totals, rows_pair, stats_pair = state
        rows_pair = from_behind((rows_pair[0], rows_pair[1]), "seq", -1)
        stats_pair = from_behind((stats_pair[0], stats_pair[1]), "seq", -1)
        totals = absorb(totals, rows_pair, stats_pair, shard_id + step)
        return (totals, rows_pair, stats_pair)

    key_grads, unused_rows, unused_stats = lax.fori_loop(
        1, shards // 2 + 1, one_hop, (start_totals, first_rows, first_stats)
    )
    query_back = (
        inverse_rotation(grad_piece, row_cos, row_sin)
        .astype(jnp.bfloat16)
        .reshape(local_rows, query_groups * head_dim)
    )
    key_backward = inverse_rotation(key_grads[:, 0:1, :], own_cos, own_sin)[:, 0, :].astype(
        jnp.bfloat16
    )
    value_backward = key_grads[:, 1, :].astype(jnp.bfloat16)
    partial_grads = (
        dot_back(query_back, w_query)
        + dot_back(key_backward, w_key)
        + dot_back(value_backward, value_weight)
    )
    grad_tokens = lax.psum_scatter(
        partial_grads.astype(jnp.bfloat16), "tp", scatter_dimension=1, tiled=True
    )
    return (output, grad_tokens)


def solution(mesh):
    return jax.shard_map(
        local,
        mesh=mesh,
        in_specs=(
            P("seq", "tp"),
            P(None, "tp"),
            P("tp"),
            P(None, "tp"),
            P("tp"),
            P(None, "tp"),
            P("tp"),
            P("tp", None),
            P(),
            P("seq", "tp"),
        ),
        out_specs=(P("seq", "tp"), P("seq", "tp")),
        check_vma=False,
    )
```

profile of v0, /device:TPU:64, one launch (start us, length us, event | category | flops | bytes accessed | tf_op | source)
XLA Modules:
  0.0 712.9 jit_solution(4178183781587554108)
XLA Ops:
  12.3 34.3 %all-gather.4.cloned.1.call-done = bf16[256,5120]{1,0:T(8,128)(2,1)} async-done(((bf16[256,1280]{1,0:T(8,128)(2,1)}), bf16[256,5120]{1,0:T(8,128)(2,1)}) %all-gather.4.cloned.1.call-update) | async-done | bytes 2621456 | tf_op jit(solution)/shard_map/all_gather | solution.py:211
  54.0 6.0 convolution_add_fusion.2
  60.6 22.9 %all-gather.8.cloned.1.call-done = bf16[256,5120]{1,0:T(8,128)(2,1)} async-done(((bf16[256,1280]{1,0:T(8,128)(2,1)}), bf16[256,5120]{1,0:T(8,128)(2,1)}) %all-gather.8.cloned.1.call-update) | async-done | bytes 2621456 | tf_op jit(solution)/shard_map/all_gather | solution.py:212
  83.6 5.9 convolution_convert_fusion.1
  91.3 42.8 %all-gather.6.cloned.1.call-done = bf16[8192,2,128]{0,2,1:T(8,128)(2,1)} async-done(((bf16[256,2,128]{0,2,1:T(8,128)(2,1)}), bf16[8192,2,128]{0,2,1:T(8,128)(2,1)}) %all-gather.6.cloned.1.call-update) | async-done | bytes 4194320 | tf_op jit(solution)/shard_map/all_gather | solution.py:234
  134.2 6.3 copy.54
  141.4 48.4 %while.54 = (s32[]{:T(128)}, f32[5,256]{1,0:T(8,128)S(1)}, f32[5,256]{1,0:T(8,128)S(1)}, f32[5,256,128]{2,1,0:T(8,128)}, s32[16]{0:T(128)S(1)}, /*index=5*/s32[]...) while((s32[]{:T(128)}, f32[5,256]{1,0:T(8,128)S(1)}, ...), condition=%wide.region_10.11_spmd.clone, body=%wide.region_4.10_spmd.clone.sunk | while | flops 343487232 | bytes 20872672 | solution.py:124
  164.3 7.6 %conditional.11 = ((f32[5,256]{1,0:T(8,128)S(1)}, f32[5,256]{1,0:T(8,128)S(1)}, f32[5,256,128]{2,1,0:T(8,128)})) conditional(s32[]{:T(128)} %convert_element_type.167, (f32[5,256]{1,0:T(8,128)S(1)}, f32[5,256]{1,0:T(8,128)S(1)}, f32[5,256,128]{2,1,0:T(8,128)}) %tuple.126, (s32[]{:T(128)}, s32[]{:T(128)}, s32[4]{0:T(128)S(1)}, s32[4]{0:T(128)S(1)}, ...), branch_computations={%region_5.5_spmd, %region_6.9_spmd} | conditional | flops 343487232 | bytes 20871326 | solution.py:117
  195.9 6.2 conditional.4
  202.1 328.6 %while.56 = (s32[]{:T(128)}, f32[256,2,128]{2,0,1:T(8,128)S(1)}, bf16[256,5,128]{2,0,1:T(8,128)(2,1)}, bf16[256,5,128]{2,0,1:T(8,128)(2,1)S(1)}, f32[5,256]{1,0:...) while((s32[]{:T(128)}, f32[256,2,128]{2,0,1:T(8,128)S(1)}, ...), condition=%wide.region_25.26_spmd.clone, body=%wide.region_20.25_spmd.clone.sunk | while | flops 338204416 | bytes 10591799 | solution.py:307
  202.1 57.2 %collective-permute-start = (bf16[256,5,128]{2,0,1:T(8,128)(2,1)}, bf16[256,5,128]{2,0,1:T(8,128)(2,1)S(1)}, u32[]{:S(2)}, u32[]{:S(2)}) collective-permute-start(bf16[256,5,128]{2,0,1:T(8,128)(2,1)} %get-tuple-element.1260), channel_id=1, source_target_pairs={{4,0},{8,4},{12,8},{16,12},{20,16},{24,20},{28,24},{32,28},{36,32}... | collective-permute-start | bytes 983048 | tf_op jit(solution)/shard_map/while/body/eval_jaxpr/ppermute | solution.py:13
  400.1 5.9 collective-permute-start
  416.5 5.9 collective-permute-start
  432.8 5.9 collective-permute-start
  449.1 5.9 collective-permute-start
  465.4 5.9 collective-permute-start
  481.8 5.9 collective-permute-start
  498.1 5.9 collective-permute-start
  514.4 5.9 collective-permute-start
  532.0 47.4 %while.55 = (s32[]{:T(128)}, f32[256,5,128]{0,2,1:T(8,128)S(1)}, s32[16]{0:T(128)S(1)}, s32[]{:T(128)}, s32[]{:T(128)}, /*index=5*/bf16[8192,2,128]{2,0,1:T(8,12...) while((s32[]{:T(128)}, f32[256,5,128]{0,2,1:T(8,128)S(1)}, ...), condition=%wide.region_17.18_spmd.clone, body=%wide.region_13.17_spmd.clone.sunk | while | flops 507980032 | bytes 9208437 | solution.py:186
  554.9 6.6 conditional.12
  589.5 6.6 convolution_convert_fusion
  596.1 73.7 %reduce-scatter.5.cloned.1.call-done = bf16[256,1280]{1,0:T(8,128)(2,1)} async-done(((bf16[256,5120]{1,0:T(8,128)(2,1)}), bf16[256,1280]{1,0:T(8,128)(2,1)}) %reduce-scatter.5.cloned.1.call-update) | async-done | bytes 655376 | tf_op jit(solution)/shard_map/reduce_scatter | solution.py:324
  669.8 36.6 %reduce-scatter.3.cloned.1.call-done = bf16[256,1280]{1,0:T(8,128)(2,1)} async-done(((bf16[256,5120]{1,0:T(8,128)(2,1)}), bf16[256,1280]{1,0:T(8,128)(2,1)}) %reduce-scatter.3.cloned.1.call-update) | async-done | bytes 655376 | tf_op jit(solution)/shard_map/reduce_scatter | solution.py:245
  (529 shorter events, 320.4 us)
Async XLA Ops:
  7.2 39.4 %all-gather.4.cloned.1.call-start = ((), (), s32[]{:S(2)}) async-start(), calls=%async_computation.2 | async-start | bytes 3276800 | tf_op jit(solution)/shard_map/all_gather | solution.py:211
  7.9 75.6 %all-gather.8.cloned.1.call-start = ((), (), s32[]{:S(2)}) async-start(), calls=%async_computation.5 | async-start | bytes 3276800 | tf_op jit(solution)/shard_map/all_gather | solution.py:212
  8.7 125.5 %all-gather.6.cloned.1.call-start = ((), (), s32[]{:S(2)}) async-start(), calls=%async_computation.3 | async-start | bytes 4325376 | tf_op jit(solution)/shard_map/all_gather | solution.py:234
  51.6 618.3 %reduce-scatter.5.cloned.1.call-start = ((), (), s32[]{:S(2)}) async-start(), calls=%async_computation.6 | async-start | bytes 3276800 | tf_op jit(solution)/shard_map/reduce_scatter | solution.py:324
  202.1 66.7 %collective-permute-start = (bf16[256,5,128]{2,0,1:T(8,128)(2,1)}, bf16[256,5,128]{2,0,1:T(8,128)(2,1)S(1)}, u32[]{:S(2)}, u32[]{:S(2)}) collective-permute-start(bf16[256,5,128]{2,0,1:T(8,128)(2,1)} %get-tuple-element.1260), channel_id=1, source_target_pairs={{4,0},{8,4},{12,8},{16,12},{20,16},{24,20},{28,24},{32,28},{36,32}... | collective-permute-start | bytes 983048 | tf_op jit(solution)/shard_map/while/body/eval_jaxpr/ppermute | solution.py:13
  274.9 13.1 %collective-permute-start = (bf16[256,5,128]{2,0,1:T(8,128)(2,1)}, bf16[256,5,128]{2,0,1:T(8,128)(2,1)S(1)}, u32[]{:S(2)}, u32[]{:S(2)}) collective-permute-start(bf16[256,5,128]{2,0,1:T(8,128)(2,1)} %get-tuple-element.1260), channel_id=1, source_target_pairs={{4,0},{8,4},{12,8},{16,12},{20,16},{24,20},{28,24},{32,28},{36,32}... | collective-permute-start | bytes 983048 | tf_op jit(solution)/shard_map/while/body/eval_jaxpr/ppermute | solution.py:13
  294.0 13.4 %collective-permute-start = (bf16[256,5,128]{2,0,1:T(8,128)(2,1)}, bf16[256,5,128]{2,0,1:T(8,128)(2,1)S(1)}, u32[]{:S(2)}, u32[]{:S(2)}) collective-permute-start(bf16[256,5,128]{2,0,1:T(8,128)(2,1)} %get-tuple-element.1260), channel_id=1, source_target_pairs={{4,0},{8,4},{12,8},{16,12},{20,16},{24,20},{28,24},{32,28},{36,32}... | collective-permute-start | bytes 983048 | tf_op jit(solution)/shard_map/while/body/eval_jaxpr/ppermute | solution.py:13
  295.9 11.5 %collective-permute-start.2 = (bf16[256,5,128]{2,0,1:T(8,128)(2,1)S(1)}, bf16[256,5,128]{2,0,1:T(8,128)(2,1)S(1)}, u32[]{:S(2)}, u32[]{:S(2)}) collective-permute-start(bf16[256,5,128]{2,0,1:T(8,128)(2,1)S(1)} %get-tuple-element.1261), channel_id=1, source_target_pairs={{4,0},{8,4},{12,8},{16,12},{20,16},{24,20},{28,24},{32,28},{36,32}... | collective-permute-start | bytes 983048 | tf_op jit(solution)/shard_map/while/body/eval_jaxpr/ppermute | solution.py:13
  313.4 11.5 %collective-permute-start = (bf16[256,5,128]{2,0,1:T(8,128)(2,1)}, bf16[256,5,128]{2,0,1:T(8,128)(2,1)S(1)}, u32[]{:S(2)}, u32[]{:S(2)}) collective-permute-start(bf16[256,5,128]{2,0,1:T(8,128)(2,1)} %get-tuple-element.1260), channel_id=1, source_target_pairs={{4,0},{8,4},{12,8},{16,12},{20,16},{24,20},{28,24},{32,28},{36,32}... | collective-permute-start | bytes 983048 | tf_op jit(solution)/shard_map/while/body/eval_jaxpr/ppermute | solution.py:13
  330.9 12.1 %collective-permute-start = (bf16[256,5,128]{2,0,1:T(8,128)(2,1)}, bf16[256,5,128]{2,0,1:T(8,128)(2,1)S(1)}, u32[]{:S(2)}, u32[]{:S(2)}) collective-permute-start(bf16[256,5,128]{2,0,1:T(8,128)(2,1)} %get-tuple-element.1260), channel_id=1, source_target_pairs={{4,0},{8,4},{12,8},{16,12},{20,16},{24,20},{28,24},{32,28},{36,32}... | collective-permute-start | bytes 983048 | tf_op jit(solution)/shard_map/while/body/eval_jaxpr/ppermute | solution.py:13
  349.0 13.4 %collective-permute-start = (bf16[256,5,128]{2,0,1:T(8,128)(2,1)}, bf16[256,5,128]{2,0,1:T(8,128)(2,1)S(1)}, u32[]{:S(2)}, u32[]{:S(2)}) collective-permute-start(bf16[256,5,128]{2,0,1:T(8,128)(2,1)} %get-tuple-element.1260), channel_id=1, source_target_pairs={{4,0},{8,4},{12,8},{16,12},{20,16},{24,20},{28,24},{32,28},{36,32}... | collective-permute-start | bytes 983048 | tf_op jit(solution)/shard_map/while/body/eval_jaxpr/ppermute | solution.py:13
  350.9 11.5 %collective-permute-start.2 = (bf16[256,5,128]{2,0,1:T(8,128)(2,1)S(1)}, bf16[256,5,128]{2,0,1:T(8,128)(2,1)S(1)}, u32[]{:S(2)}, u32[]{:S(2)}) collective-permute-start(bf16[256,5,128]{2,0,1:T(8,128)(2,1)S(1)} %get-tuple-element.1261), channel_id=1, source_target_pairs={{4,0},{8,4},{12,8},{16,12},{20,16},{24,20},{28,24},{32,28},{36,32}... | collective-permute-start | bytes 983048 | tf_op jit(solution)/shard_map/while/body/eval_jaxpr/ppermute | solution.py:13
  368.4 13.4 %collective-permute-start = (bf16[256,5,128]{2,0,1:T(8,128)(2,1)}, bf16[256,5,128]{2,0,1:T(8,128)(2,1)S(1)}, u32[]{:S(2)}, u32[]{:S(2)}) collective-permute-start(bf16[256,5,128]{2,0,1:T(8,128)(2,1)} %get-tuple-element.1260), channel_id=1, source_target_pairs={{4,0},{8,4},{12,8},{16,12},{20,16},{24,20},{28,24},{32,28},{36,32}... | collective-permute-start | bytes 983048 | tf_op jit(solution)/shard_map/while/body/eval_jaxpr/ppermute | solution.py:13
  370.3 11.5 %collective-permute-start.2 = (bf16[256,5,128]{2,0,1:T(8,128)(2,1)S(1)}, bf16[256,5,128]{2,0,1:T(8,128)(2,1)S(1)}, u32[]{:S(2)}, u32[]{:S(2)}) collective-permute-start(bf16[256,5,128]{2,0,1:T(8,128)(2,1)S(1)} %get-tuple-element.1261), channel_id=1, source_target_pairs={{4,0},{8,4},{12,8},{16,12},{20,16},{24,20},{28,24},{32,28},{36,32}... | collective-permute-start | bytes 983048 | tf_op jit(solution)/shard_map/while/body/eval_jaxpr/ppermute | solution.py:13
  387.8 11.5 %collective-permute-start = (bf16[256,5,128]{2,0,1:T(8,128)(2,1)}, bf16[256,5,128]{2,0,1:T(8,128)(2,1)S(1)}, u32[]{:S(2)}, u32[]{:S(2)}) collective-permute-start(bf16[256,5,128]{2,0,1:T(8,128)(2,1)} %get-tuple-element.1260), channel_id=1, source_target_pairs={{4,0},{8,4},{12,8},{16,12},{20,16},{24,20},{28,24},{32,28},{36,32}... | collective-permute-start | bytes 983048 | tf_op jit(solution)/shard_map/while/body/eval_jaxpr/ppermute | solution.py:13
  400.1 15.5 %collective-permute-start = (bf16[256,5,128]{2,0,1:T(8,128)(2,1)}, bf16[256,5,128]{2,0,1:T(8,128)(2,1)S(1)}, u32[]{:S(2)}, u32[]{:S(2)}) collective-permute-start(bf16[256,5,128]{2,0,1:T(8,128)(2,1)} %get-tuple-element.1260), channel_id=1, source_target_pairs={{4,0},{8,4},{12,8},{16,12},{20,16},{24,20},{28,24},{32,28},{36,32}... | collective-permute-start | bytes 983048 | tf_op jit(solution)/shard_map/while/body/eval_jaxpr/ppermute | solution.py:13
  416.5 15.5 %collective-permute-start = (bf16[256,5,128]{2,0,1:T(8,128)(2,1)}, bf16[256,5,128]{2,0,1:T(8,128)(2,1)S(1)}, u32[]{:S(2)}, u32[]{:S(2)}) collective-permute-start(bf16[256,5,128]{2,0,1:T(8,128)(2,1)} %get-tuple-element.1260), channel_id=1, source_target_pairs={{4,0},{8,4},{12,8},{16,12},{20,16},{24,20},{28,24},{32,28},{36,32}... | collective-permute-start | bytes 983048 | tf_op jit(solution)/shard_map/while/body/eval_jaxpr/ppermute | solution.py:13
  432.8 15.5 %collective-permute-start = (bf16[256,5,128]{2,0,1:T(8,128)(2,1)}, bf16[256,5,128]{2,0,1:T(8,128)(2,1)S(1)}, u32[]{:S(2)}, u32[]{:S(2)}) collective-permute-start(bf16[256,5,128]{2,0,1:T(8,128)(2,1)} %get-tuple-element.1260), channel_id=1, source_target_pairs={{4,0},{8,4},{12,8},{16,12},{20,16},{24,20},{28,24},{32,28},{36,32}... | collective-permute-start | bytes 983048 | tf_op jit(solution)/shard_map/while/body/eval_jaxpr/ppermute | solution.py:13
  449.1 15.5 %collective-permute-start = (bf16[256,5,128]{2,0,1:T(8,128)(2,1)}, bf16[256,5,128]{2,0,1:T(8,128)(2,1)S(1)}, u32[]{:S(2)}, u32[]{:S(2)}) collective-permute-start(bf16[256,5,128]{2,0,1:T(8,128)(2,1)} %get-tuple-element.1260), channel_id=1, source_target_pairs={{4,0},{8,4},{12,8},{16,12},{20,16},{24,20},{28,24},{32,28},{36,32}... | collective-permute-start | bytes 983048 | tf_op jit(solution)/shard_map/while/body/eval_jaxpr/ppermute | solution.py:13
  465.4 15.5 %collective-permute-start = (bf16[256,5,128]{2,0,1:T(8,128)(2,1)}, bf16[256,5,128]{2,0,1:T(8,128)(2,1)S(1)}, u32[]{:S(2)}, u32[]{:S(2)}) collective-permute-start(bf16[256,5,128]{2,0,1:T(8,128)(2,1)} %get-tuple-element.1260), channel_id=1, source_target_pairs={{4,0},{8,4},{12,8},{16,12},{20,16},{24,20},{28,24},{32,28},{36,32}... | collective-permute-start | bytes 983048 | tf_op jit(solution)/shard_map/while/body/eval_jaxpr/ppermute | solution.py:13
  481.8 15.5 %collective-permute-start = (bf16[256,5,128]{2,0,1:T(8,128)(2,1)}, bf16[256,5,128]{2,0,1:T(8,128)(2,1)S(1)}, u32[]{:S(2)}, u32[]{:S(2)}) collective-permute-start(bf16[256,5,128]{2,0,1:T(8,128)(2,1)} %get-tuple-element.1260), channel_id=1, source_target_pairs={{4,0},{8,4},{12,8},{16,12},{20,16},{24,20},{28,24},{32,28},{36,32}... | collective-permute-start | bytes 983048 | tf_op jit(solution)/shard_map/while/body/eval_jaxpr/ppermute | solution.py:13
  498.1 15.5 %collective-permute-start = (bf16[256,5,128]{2,0,1:T(8,128)(2,1)}, bf16[256,5,128]{2,0,1:T(8,128)(2,1)S(1)}, u32[]{:S(2)}, u32[]{:S(2)}) collective-permute-start(bf16[256,5,128]{2,0,1:T(8,128)(2,1)} %get-tuple-element.1260), channel_id=1, source_target_pairs={{4,0},{8,4},{12,8},{16,12},{20,16},{24,20},{28,24},{32,28},{36,32}... | collective-permute-start | bytes 983048 | tf_op jit(solution)/shard_map/while/body/eval_jaxpr/ppermute | solution.py:13
  514.4 15.5 %collective-permute-start = (bf16[256,5,128]{2,0,1:T(8,128)(2,1)}, bf16[256,5,128]{2,0,1:T(8,128)(2,1)S(1)}, u32[]{:S(2)}, u32[]{:S(2)}) collective-permute-start(bf16[256,5,128]{2,0,1:T(8,128)(2,1)} %get-tuple-element.1260), channel_id=1, source_target_pairs={{4,0},{8,4},{12,8},{16,12},{20,16},{24,20},{28,24},{32,28},{36,32}... | collective-permute-start | bytes 983048 | tf_op jit(solution)/shard_map/while/body/eval_jaxpr/ppermute | solution.py:13
  588.5 117.9 %reduce-scatter.3.cloned.1.call-start = ((), (), s32[]{:S(2)}) async-start(), calls=%async_computation.4 | async-start | bytes 3276800 | tf_op jit(solution)/shard_map/reduce_scatter | solution.py:245
  (73 other events, 689.7 us)
Sparse Core Ops, SparseCore 0:
  9.7 36.8 all-gather.3
  48.2 35.2 all-gather.7
  86.3 47.7 all-gather.5
  588.6 81.1 reduce-scatter.4
  672.6 33.7 reduce-scatter.2
where the time goes:
time: 720 us; the launch traced here: 713 us
  waiting for transfers between devices  224 us (31%)
  starting transfers between devices  215 us (30%)
  loops' own time  74.9 us (10%)
  matrix products  73.2 us (10%)
  local copies, waits for them, and re-layouts  71.1 us (10%)
  other arithmetic  40.1 us (6%)
  between operations  14.8 us (2%)
    ppermute x64, starting transfers between devices, from_behind(): return lax.ppermute(value, axis, pairs)  215 us
    reduce_scatter x1, waiting for transfers between devices, local(): lax.psum_scatter(partial_grads.astype(jnp.bfloat16), 'tp', scatter_dimens...  73.7 us
    all_gather x1, waiting for transfers between devices, local(): all_pairs = lax.all_gather(own_pairs, 'seq', axis=0, tiled=True)  42.8 us
    reduce_scatter x1, waiting for transfers between devices, local(): lax.psum_scatter(partial_out.astype(jnp.bfloat16), 'tp', scatter_dimensio...  36.6 us
    all_gather x1, waiting for transfers between devices, local(): lax.all_gather(tokens, 'tp', axis=1, tiled=True)  34.3 us
    while x64, local copies, waits for them, and re-layouts  31.4 us
    another operation x1, loops' own time, query_grads(): lax.scan(query_one_span, start_state, jnp.arange(key_total // key_span))  31.2 us
    another operation x1, loops' own time, attend(): lax.scan(attend_one_span, start_state, jnp.arange(all_pairs.shape[0] // k...  30.6 us
  transfers between devices with their start and end apart: 69, of which 22 were waited for; matrix products, arithmetic and copies ran while one was open for 10% of the time, Pallas kernels for 0%

commit v1 on v0

v1 whole, which is shorter than its diff:
```python
import functools

import jax
import jax.numpy as jnp
from jax import lax
from jax.experimental import pallas as pl
from jax.experimental.pallas import tpu as pltpu
from jax.sharding import PartitionSpec as P

theta_base = 1000000.0
neg_large = -1e30
log2e = 1.4426950408889634
HEAD = 128
F32 = jnp.float32
BF16 = jnp.bfloat16


def start_of(token_index, doc_starts, doc_ends):
    inside = (token_index[:, None] >= doc_starts[None, :]) & (
        token_index[:, None] < doc_ends[None, :]
    )
    return jnp.sum(jnp.where(inside, doc_starts[None, :], 0), axis=1)


def rope_tables(position):
    half = HEAD // 2
    frequency = theta_base ** (-2.0 * jnp.arange(half, dtype=F32) / HEAD)
    angles = position.astype(F32)[:, None] * frequency[None, :]
    cos, sin = jnp.cos(angles), jnp.sin(angles)
    return jnp.concatenate([cos, cos], axis=1), jnp.concatenate([-sin, sin], axis=1)


def swap_halves(u):
    return jnp.concatenate([u[:, HEAD // 2 :], u[:, : HEAD // 2]], axis=1)


def nn(a, b):
    return lax.dot_general(a, b, (((1,), (0,)), ((), ())), preferred_element_type=F32)


def nt(a, b):
    return lax.dot_general(a, b, (((1,), (1,)), ((), ())), preferred_element_type=F32)


def key_mask(block, rows, first_key, row_index):
    key_index = block * rows + lax.broadcasted_iota(jnp.int32, (rows, rows), 0)
    return (key_index >= first_key) & (key_index <= row_index)


def forward_kernel(meta_ref, start_ref, q_ref, kv_ref, o_ref, lse_ref, qt, m_s, l_s, acc):
    groups, rows, _ = q_ref.shape
    mine, low = meta_ref[0], meta_ref[1]
    scale = HEAD**-0.5 * log2e
    first_key = start_ref[...]
    row_index = mine * rows + lax.broadcasted_iota(jnp.int32, (1, rows), 1)
    for h in range(groups):
        qt[h] = q_ref[h].T

    def block_step(block, first):
        k = kv_ref[block, :, :HEAD]
        vt = kv_ref[block, :, HEAD:].T
        allowed = key_mask(block, rows, first_key, row_index)
        for h in range(groups):
            s = jnp.where(allowed, nn(k, qt[h]) * scale, neg_large)
            top = jnp.max(s, axis=0, keepdims=True)
            if not first:
                old = m_s[pl.ds(h, 1), :]
                top = jnp.maximum(old, top)
            p = jnp.exp2(s - top)
            mass = jnp.sum(p, axis=0, keepdims=True)
            part = nn(vt, p.astype(BF16))
            if first:
                acc[h] = part
            else:
                shrink = jnp.exp2(old - top)
                mass = mass + l_s[pl.ds(h, 1), :] * shrink
                acc[h] = acc[h] * shrink + part
            l_s[pl.ds(h, 1), :] = mass
            m_s[pl.ds(h, 1), :] = top

    block_step(mine, True)

    def body(i, _):
        block_step(mine - i, False)
        return 0

    lax.fori_loop(1, mine - low + 1, body, 0)
    for h in range(groups):
        mass = l_s[pl.ds(h, 1), :]
        o_ref[:, h * HEAD : (h + 1) * HEAD] = (acc[h] / mass).T.astype(BF16)
        lse_ref[pl.ds(h, 1), :] = m_s[pl.ds(h, 1), :] + jnp.log2(mass)


def backward_kernel(
    meta_ref, start_ref, q_ref, g_ref, o_ref, lse_ref, kv_ref, cos_ref, sin_ref,
    dq_ref, dkv_ref, qt, gt, delta_s, dqt,
):
    groups, rows, _ = q_ref.shape
    mine, low = meta_ref[0], meta_ref[1]
    factor = HEAD**-0.5
    scale = factor * log2e
    first_key = start_ref[...]
    row_index = mine * rows + lax.broadcasted_iota(jnp.int32, (1, rows), 1)
    for h in range(groups):
        cols = slice(h * HEAD, (h + 1) * HEAD)
        g_t = g_ref[:, cols].astype(F32).T
        o_t = o_ref[:, cols].astype(F32).T
        qt[h] = q_ref[h].T
        gt[h] = g_t.astype(BF16)
        delta_s[pl.ds(h, 1), :] = jnp.sum(g_t * o_t, axis=0, keepdims=True)
        dqt[h] = jnp.zeros_like(dqt[h])

    def zero(b, _):
        dkv_ref[b] = jnp.zeros_like(dkv_ref[b])
        return 0

    lax.fori_loop(0, low, zero, 0)
    lax.fori_loop(mine + 1, dkv_ref.shape[0], zero, 0)

    def body(i, _):
        block = low + i
        k = kv_ref[block, :, :HEAD]
        v = kv_ref[block, :, HEAD:]
        kt = k.T
        allowed = key_mask(block, rows, first_key, row_index)
        dk = jnp.zeros((rows, HEAD), F32)
        dv = jnp.zeros((rows, HEAD), F32)
        for h in range(groups):
            s = nn(k, qt[h]) * scale
            p = jnp.where(allowed, jnp.exp2(s - lse_ref[pl.ds(h, 1), :]), 0.0)
            ds = p * (nn(v, gt[h]) - delta_s[pl.ds(h, 1), :])
            pb, dsb = p.astype(BF16), ds.astype(BF16)
            dv = dv + nn(pb, g_ref[:, h * HEAD : (h + 1) * HEAD])
            dk = dk + nn(dsb, q_ref[h])
            dqt[h] = dqt[h] + nn(kt, dsb)
        dkv_ref[block, :, :HEAD] = (dk * factor).astype(BF16)
        dkv_ref[block, :, HEAD:] = dv.astype(BF16)
        return 0

    lax.fori_loop(0, mine - low + 1, body, 0)
    cos, sin = cos_ref[...], sin_ref[...]
    for h in range(groups):
        u = dqt[h].T * factor
        dq_ref[:, h * HEAD : (h + 1) * HEAD] = (u * cos - swap_halves(u) * sin).astype(BF16)


def vmem():
    return pl.BlockSpec(memory_space=pltpu.VMEM)


def smem():
    return pl.BlockSpec(memory_space=pltpu.SMEM)


def local(
    tokens, w_query, b_query, w_key, key_bias, value_weight, value_bias, w_out, doc_lengths, grad_out
):
    shards = lax.axis_size("seq")
    mine = lax.axis_index("seq")
    rows = tokens.shape[0]
    groups = w_query.shape[1] // HEAD
    doc_ends = jnp.cumsum(doc_lengths)
    doc_starts = doc_ends - doc_lengths
    index = mine * rows + jnp.arange(rows, dtype=jnp.int32)
    start = start_of(index, doc_starts, doc_ends)
    cos, sin = rope_tables(index - start)
    full_tokens = lax.all_gather(tokens, "tp", axis=1, tiled=True)
    full_grads = lax.all_gather(grad_out, "tp", axis=1, tiled=True)

    def rotated(raw, bias):
        u = (raw + bias.astype(F32)).reshape(rows, -1, HEAD)
        swapped = jnp.concatenate([u[..., HEAD // 2 :], u[..., : HEAD // 2]], axis=-1)
        return (u * cos[:, None] + swapped * sin[:, None]).astype(BF16)

    key = rotated(nn(full_tokens, w_key), key_bias)[:, 0]
    value = (nn(full_tokens, value_weight) + value_bias.astype(F32)).astype(BF16)
    query = jnp.transpose(rotated(nn(full_tokens, w_query), b_query), (1, 0, 2))
    pair = jnp.concatenate([key, value], axis=1)
    pairs = lax.all_gather(pair, "seq", axis=0, tiled=False)
    grad_attended = nt(full_grads, w_out).astype(BF16)
    meta = jnp.stack([mine, start[0] // rows]).astype(jnp.int32)
    start_row = start[None, :].astype(jnp.int32)
    stats = jax.ShapeDtypeStruct((8, rows), F32)
    params = pltpu.CompilerParams(vmem_limit_bytes=48 << 20)
    attended, lse = pl.pallas_call(
        forward_kernel,
        out_shape=(jax.ShapeDtypeStruct((rows, groups * HEAD), BF16), stats),
        in_specs=[smem(), vmem(), vmem(), vmem()],
        out_specs=(vmem(), vmem()),
        scratch_shapes=[
            pltpu.VMEM((groups, HEAD, rows), BF16),
            pltpu.VMEM((8, rows), F32),
            pltpu.VMEM((8, rows), F32),
            pltpu.VMEM((groups, HEAD, rows), F32),
        ],
        compiler_params=params,
        name="attention_forward",
    )(meta, start_row, query, pairs)
    output = lax.psum_scatter(
        nn(attended, w_out).astype(BF16), "tp", scatter_dimension=1, tiled=True
    )
    query_back, pair_grads = pl.pallas_call(
        backward_kernel,
        out_shape=(
            jax.ShapeDtypeStruct((rows, groups * HEAD), BF16),
            jax.ShapeDtypeStruct((shards, rows, 2 * HEAD), BF16),
        ),
        in_specs=[smem()] + [vmem()] * 8,
        out_specs=(vmem(), vmem()),
        scratch_shapes=[
            pltpu.VMEM((groups, HEAD, rows), BF16),
            pltpu.VMEM((groups, HEAD, rows), BF16),
            pltpu.VMEM((8, rows), F32),
            pltpu.VMEM((groups, HEAD, rows), F32),
        ],
        compiler_params=params,
        name="attention_backward",
    )(meta, start_row, query, grad_attended, attended, lse, pairs, cos, sin)
    own = lax.psum_scatter(pair_grads, "seq", scatter_dimension=0, tiled=False).astype(F32)
    key_grad = own[:, :HEAD]
    key_back = (key_grad * cos - swap_halves(key_grad) * sin).astype(BF16)
    value_back = own[:, HEAD:].astype(BF16)
    partial = nt(query_back, w_query) + nt(key_back, w_key) + nt(value_back, value_weight)
    grad_tokens = lax.psum_scatter(partial.astype(BF16), "tp", scatter_dimension=1, tiled=True)
    return output, grad_tokens


def solution(mesh):
    return jax.shard_map(
        local,
        mesh=mesh,
        in_specs=(
            P("seq", "tp"),
            P(None, "tp"),
            P("tp"),
            P(None, "tp"),
            P("tp"),
            P(None, "tp"),
            P("tp"),
            P("tp", None),
            P(),
            P("seq", "tp"),
        ),
        out_specs=(P("seq", "tp"), P("seq", "tp")),
        check_vma=False,
    )
```

time: 720 us -> 353 us (0.49)
  starting transfers between devices: 215 us -> 0.42 us
  loops' own time: 74.9 us -> 0 us
  local copies, waits for them, and re-layouts: 71.1 us -> 5.62 us
  waiting for transfers between devices: 224 us -> 269 us
  matrix products: 73.2 us -> 35.4 us
  other arithmetic: 40.1 us -> 5.57 us
  Pallas kernels: 0 us -> 18.5 us
    ppermute x64 -> x0, starting transfers between devices: 215 us -> none  [from_behind(): return lax.ppermute(value, axis, pairs)]
    another operation x52 -> x0, loops' own time: 74.9 us -> none  [the longest x1 31.2 us: query_grads(): lax.scan(query_one_span, start_state, jnp.arange(key_total // key_span))]
    reduce_scatter x2 -> x3, waiting for transfers between devices: 110 us -> 169 us  [the longest x1 102 us: local(): lax.psum_scatter(pair_grads, 'seq', scatter_dimension=0, tiled=False)]
    dot_general x36 -> x8, matrix products: 73.2 us -> 35.4 us  [the longest x4 19.2 us: nt(): lax.dot_general(a, b, (((1,), (1,)), ((), ())), preferred_element_type=F32)]
    while x66 -> x0, local copies, waits for them, and re-layouts: 32.9 us -> none
    dynamic_slice x32 -> x0, local copies, waits for them, and re-layouts: 19.3 us -> none  [attend(): lax.scan(attend_one_span, start_state, jnp.arange(all_pairs.shape[0] // k...]
    pallas_call x0 -> x2, Pallas kernels: none -> 18.5 us  [the longest x1 10.1 us: local(): pl.pallas_call(backward_kernel, out_shape=(jax.ShapeDtypeStruct((rows, gr...]
    reduce_sum x19 -> x1, other arithmetic: 12.2 us -> 0.09 us  [start_of(): return jnp.sum(jnp.where(inside, doc_starts[None, :], 0), axis=1)]
  transfers between devices with their start and end apart: 69 -> 6, of which waited for: 22 -> 6; matrix products, arithmetic and copies ran while one was open for 10% -> 12% of each run, Pallas kernels for 0% -> 0%
where the time goes in v1:
time: 353 us; the launch traced here: 351 us
  waiting for transfers between devices  269 us (76%)
  matrix products  35.4 us (10%)
  Pallas kernels  18.5 us (5%)
  between operations  16.8 us (5%)
  local copies, waits for them, and re-layouts  5.62 us (2%)
  other arithmetic  5.57 us (2%)
    reduce_scatter x1, waiting for transfers between devices, local(): lax.psum_scatter(pair_grads, 'seq', scatter_dimension=0, tiled=False)  102 us
    all_gather x1, waiting for transfers between devices, local(): pairs = lax.all_gather(pair, 'seq', axis=0, tiled=False)  42.1 us
    reduce_scatter x1, waiting for transfers between devices, local(): lax.psum_scatter(partial.astype(BF16), 'tp', scatter_dimension=1, tiled=T...  36.7 us
    all_gather x1, waiting for transfers between devices, local(): full_tokens = lax.all_gather(tokens, 'tp', axis=1, tiled=True)  34.4 us
    reduce_scatter x1, waiting for transfers between devices, local(): lax.psum_scatter(nn(attended, w_out).astype(BF16), 'tp', scatter_dimensio...  29.9 us
    all_gather x1, waiting for transfers between devices, local(): full_grads = lax.all_gather(grad_out, 'tp', axis=1, tiled=True)  22.1 us
    dot_general x4, matrix products, nt(): lax.dot_general(a, b, (((1,), (1,)), ((), ())), preferred_element_type=F32)  19.2 us
    dot_general x4, matrix products, nn(): lax.dot_general(a, b, (((1,), (0,)), ((), ())), preferred_element_type=F32)  16.2 us
  transfers between devices with their start and end apart: 6, of which 6 were waited for; matrix products, arithmetic and copies ran while one was open for 12% of the time, Pallas kernels for 0%

profile of v1, /device:TPU:64, one launch (start us, length us, event | category | flops | bytes accessed | tf_op | source)
XLA Modules:
  0.0 351.1 jit_solution(9922685272908656535)
XLA Ops:
  7.2 0.7 all-gather.5.cloned.1.call-update
  8.0 0.7 all-gather.7.cloned.1.call-update
  10.0 0.8 reduce-window.8
  10.9 0.7 bitcast_subtract_fusion
  12.2 34.4 %all-gather.5.cloned.1.call-done = bf16[256,5120]{1,0:T(8,128)(2,1)} async-done(((bf16[256,1280]{1,0:T(8,128)(2,1)}), bf16[256,5120]{1,0:T(8,128)(2,1)}) %all-gather.5.cloned.1.call-update) | async-done | bytes 2621456 | tf_op jit(solution)/shard_map/all_gather | solution.py:167
  46.6 2.7 convolution_add_fusion.4
  49.6 0.9 fusion.1
  50.5 0.7 pad_maximum_fusion.2
  54.3 6.1 %convolution_add_fusion.2 = f32[256,640]{1,0:T(8,128)S(1)} fusion(bf16[256,5120]{1,0:T(8,128)(2,1)} %all-gather.5.cloned.1.call-done, bf16[5120,640]{1,0:T(8,128)(2,1)} %param.11, f32[640]{0:T(1024)S(1)} %convert_element_type.45), kind=kOutput, calls=%fused_computation.4 | convolution fusion | flops 1677885440 | bytes 9832960 | tf_op jit(solution)/shard_map/dot_general | solution.py:38
  61.4 22.1 %all-gather.7.cloned.1.call-done = bf16[256,5120]{1,0:T(8,128)(2,1)} async-done(((bf16[256,1280]{1,0:T(8,128)(2,1)}), bf16[256,5120]{1,0:T(8,128)(2,1)}) %all-gather.7.cloned.1.call-update) | async-done | bytes 2621456 | tf_op jit(solution)/shard_map/all_gather | solution.py:168
  83.6 5.9 %convolution_convert_fusion.1.g_ref = bf16[256,640]{1,0:T(8,128)(2,1)S(1)} fusion(bf16[256,5120]{1,0:T(8,128)(2,1)} %all-gather.7.cloned.1.call-done, bf16[640,5120]{1,0:T(8,128)(2,1)} %param.17), kind=kOutput, calls=%fused_computation.5 | convolution fusion | flops 1677885440 | bytes 9502720 | tf_op jit(solution)/shard_map/dot_general | solution.py:42
  89.5 42.1 %all-gather.9.cloned.1.call-done = bf16[8192,256]{1,0:T(8,128)(2,1)} async-done(((bf16[256,256]{1,0:T(8,128)(2,1)}), bf16[8192,256]{1,0:T(8,128)(2,1)}) %all-gather.9.cloned.1.call-update) | async-done | bytes 4194320 | tf_op jit(solution)/shard_map/all_gather | solution.py:179
  131.6 2.2 copy-done.1
  133.8 8.4 %attention_forward.1 = (bf16[256,640]{1,0:T(8,128)(2,1)S(1)}, f32[8,256]{1,0:T(8,128)S(1)}) custom-call(s32[2]{0:T(128)S(1)} %pad_add_fusion.meta_ref, s32[1,256]{1,0:T(1,128)S(1)} %bitcast.34, bf16[5,256,128]{2,1,0:T(8,128)(2,1)S(1)} %fusion.4.q_ref, bf16[32,256,256]{2,1,0:T(8,128)(2,1)S(1)} %bitcast.33), custom_call_target="tpu_custom_call" | custom-call | tf_op jit(solution)/shard_map/attention_forward/pallas_call | solution.py:185
  142.2 10.1 %attention_backward.1 = (bf16[256,640]{1,0:T(8,128)(2,1)S(1)}, bf16[32,256,256]{2,1,0:T(8,128)(2,1)S(1)}) custom-call(s32[2]{0:T(128)S(1)} %pad_add_fusion.meta_ref, s32[1,256]{1,0:T(1,128)S(1)} %bitcast.35, bf16[5,256,128]{2,1,0:T(8,128)(2,1)S(1)} %fusion.4.q_ref, bf16[256,640]{1,0:T(8,128)(2,1)S(1)} %convolution_convert_fusion.1.g_ref, ...), custom_call_target="tpu_custom_call" | custom-call | tf_op jit(solution)/shard_map/attention_backward/pallas_call | solution.py:202
  152.3 2.0 copy-done.2
  154.6 6.6 %convolution_convert_fusion = bf16[256,5120]{1,0:T(8,128)(2,1)} fusion(bf16[256,640]{1,0:T(8,128)(2,1)S(1)} %get-tuple-element.6.o_ref, bf16[640,5120]{1,0:T(8,128)(2,1)} %param.17), kind=kOutput, calls=%fused_computation.3 | convolution fusion | flops 1679032320 | bytes 9502720 | tf_op jit(solution)/shard_map/dot_general | solution.py:38
  161.2 7.4 %fusion.15 = f32[256,5120]{1,0:T(8,128)} fusion(bf16[256,640]{1,0:T(8,128)(2,1)S(1)} %get-tuple-element.8, bf16[5120,640]{1,0:T(8,128)(2,1)} %param.11), kind=kOutput, calls=%fused_computation.39 | convolution fusion | flops 1677721600 | bytes 12124160 | tf_op jit(solution)/shard_map/dot_general | solution.py:42
  168.6 102.0 %reduce-scatter.6.cloned.1.call-done = bf16[1,256,256]{2,1,0:T(8,128)(2,1)} async-done(((bf16[32,256,256]{2,1,0:T(8,128)(2,1)}), bf16[1,256,256]{2,1,0:T(8,128)(2,1)}) %reduce-scatter.6.cloned.1.call-update) | async-done | bytes 131088 | tf_op jit(solution)/shard_map/reduce_scatter | solution.py:219
  270.7 0.9 bitcast_convert_fusion
  271.7 3.5 convolution_add_fusion.1
  275.2 2.4 fusion
  277.6 29.9 %reduce-scatter.4.cloned.1.call-done = bf16[256,1280]{1,0:T(8,128)(2,1)} async-done(((bf16[256,5120]{1,0:T(8,128)(2,1)}), bf16[256,1280]{1,0:T(8,128)(2,1)}) %reduce-scatter.4.cloned.1.call-update) | async-done | bytes 655376 | tf_op jit(solution)/shard_map/reduce_scatter | solution.py:199
  307.5 36.7 %reduce-scatter.8.cloned.1.call-done = bf16[256,1280]{1,0:T(8,128)(2,1)} async-done(((bf16[256,5120]{1,0:T(8,128)(2,1)}), bf16[256,1280]{1,0:T(8,128)(2,1)}) %reduce-scatter.8.cloned.1.call-update) | async-done | bytes 655376 | tf_op jit(solution)/shard_map/reduce_scatter | solution.py:224
  (41 shorter events, 4.4 us)
Async XLA Ops:
  7.2 39.4 %copy-start = (bf16[5120,128]{1,0:T(8,128)(2,1)S(1)}, bf16[5120,128]{1,0:T(8,128)(2,1)}, u32[]{:S(2)}) copy-start(bf16[5120,128]{1,0:T(8,128)(2,1)} %param.13) | copy-start | bytes 3932164
  7.2 39.4 %all-gather.5.cloned.1.call-start = ((), (), s32[]{:S(2)}) async-start(), calls=%async_computation.3 | async-start | bytes 3276800 | tf_op jit(solution)/shard_map/all_gather | solution.py:167
  7.9 75.6 %all-gather.7.cloned.1.call-start = ((), (), s32[]{:S(2)}) async-start(), calls=%async_computation.5 | async-start | bytes 3276800 | tf_op jit(solution)/shard_map/all_gather | solution.py:168
  8.7 122.9 %all-gather.9.cloned.1.call-start = ((), (), s32[]{:S(2)}) async-start(), calls=%async_computation.8 | async-start | bytes 4325376 | tf_op jit(solution)/shard_map/all_gather | solution.py:179
  12.2 37.4 %copy-start.4 = (bf16[5120,128]{1,0:T(8,128)(2,1)S(1)}, bf16[5120,128]{1,0:T(8,128)(2,1)}, u32[]{:S(2)}) copy-start(bf16[5120,128]{1,0:T(8,128)(2,1)} %param.15) | copy-start | bytes 3932164
  46.6 3.0 copy-start.3
  49.4 4.8 %copy-start.7 = (bf16[640]{0:T(1024)(128)(2,1)S(1)}, bf16[640]{0:T(1024)(128)(2,1)}, u32[]{:S(2)}) copy-start(bf16[640]{0:T(1024)(128)(2,1)} %param.12) | copy-start | bytes 3844
  51.2 219.5 %reduce-scatter.6.cloned.1.call-start = ((), (), s32[]{:S(2)}) async-start(), calls=%async_computation.6 | async-start | bytes 4325376 | tf_op jit(solution)/shard_map/reduce_scatter | solution.py:219
  131.6 2.2 copy-start.1
  152.3 2.0 copy-start.2
  154.4 153.2 %reduce-scatter.4.cloned.1.call-start = ((), (), s32[]{:S(2)}) async-start(), calls=%async_computation.4 | async-start | bytes 3276800 | tf_op jit(solution)/shard_map/reduce_scatter | solution.py:199
  161.2 183.1 %reduce-scatter.8.cloned.1.call-start = ((), (), s32[]{:S(2)}) async-start(), calls=%async_computation.7 | async-start | bytes 3276800 | tf_op jit(solution)/shard_map/reduce_scatter | solution.py:224
  271.7 3.5 %copy-start.5 = (bf16[5120,128]{1,0:T(8,128)(2,1)S(1)}, bf16[5120,128]{1,0:T(8,128)(2,1)}, u32[]{:S(2)}) copy-start(bf16[5120,128]{1,0:T(8,128)(2,1)} %param.15) | copy-start | bytes 3932164
  271.7 3.5 %copy-start.6 = (bf16[1,256,256]{2,1,0:T(8,128)(2,1)S(1)}, bf16[1,256,256]{2,1,0:T(8,128)(2,1)}, u32[]{:S(2)}) copy-start(bf16[1,256,256]{2,1,0:T(8,128)(2,1)} %reduce-scatter.6.cloned.1.call-done) | copy-start | bytes 393220
Sparse Core Ops, SparseCore 0:
  9.7 36.8 all-gather.4
  48.2 35.2 all-gather.6
  86.4 45.1 all-gather.8
  154.5 116.1 reduce-scatter.5
  273.6 33.8 reduce-scatter.3
  310.5 33.6 reduce-scatter.7

commit v2 on v1

v2 whole, which is shorter than its diff:
```python
import functools

import jax
import jax.numpy as jnp
from jax import lax
from jax.experimental import pallas as pl
from jax.experimental.pallas import tpu as pltpu
from jax.sharding import PartitionSpec as P

theta_base = 1000000.0
neg_large = -1e30
log2e = 1.4426950408889634
HEAD = 128
ROWS = 256
HALF = 128
CHUNK = 64
HEADS = 5
WIDTH = 1280
FEAT = HEADS * HEAD
CHIPS = 16
REACH = 8
F32 = jnp.float32
BF16 = jnp.bfloat16
MESH = pl.DeviceIdType.MESH
factor = HEAD**-0.5
scale = factor * log2e


def start_of(token_index, doc_starts, doc_ends):
    inside = (token_index[:, None] >= doc_starts[None, :]) & (
        token_index[:, None] < doc_ends[None, :]
    )
    return jnp.sum(jnp.where(inside, doc_starts[None, :], 0), axis=1)


def rope_tables(position):
    half = HEAD // 2
    frequency = theta_base ** (-2.0 * jnp.arange(half, dtype=F32) / HEAD)
    angles = position.astype(F32)[:, None] * frequency[None, :]
    cos, sin = jnp.cos(angles), jnp.sin(angles)
    return jnp.concatenate([cos, cos], axis=1), jnp.concatenate([-sin, sin], axis=1)


def nn(a, b):
    return lax.dot_general(a, b, (((1,), (0,)), ((), ())), preferred_element_type=F32)


def nt(a, b):
    return lax.dot_general(a, b, (((1,), (1,)), ((), ())), preferred_element_type=F32)


def block_kernel(
    tok, grad, wq_hbm, wk_hbm, wv_hbm, wo_hbm, bias, cos_ref, sin_ref, start_ref,
    out_ref, gtok_ref,
    w, wo, tk, gr, acc, gacc, qn, qt, gn, gt, kv, at, att, oacc, m_s, l_s, lse, delta,
    tmp, own, sib_out, sib_in, dkv_out, dkv_in, x, p_out, v_out, f_out, p_grad, v_grad, f_grad,
    wsem, ys, yr, fs, fr, kvs, kvr, sbs, sbr, dss, dsr, dos, dor, rss, rsr,
):
    s = lax.axis_index("seq")
    t = lax.axis_index("tp")
    chip, core = lax.div(s, 2), lax.rem(s, 2)
    right, left, opp = lax.rem(t + 1, 4), lax.rem(t + 3, 4), lax.rem(t + 2, 4)
    to_right, to_left = {"seq": s, "tp": right}, {"seq": s, "tp": left}
    sibling = {"seq": s + 1 - 2 * core, "tp": t}

    def remote(src, dst, send, recv, device):
        return pltpu.make_async_remote_copy(
            src_ref=src, dst_ref=dst, send_sem=send, recv_sem=recv,
            device_id=device, device_id_type=MESH,
        )

    loads = []
    for i in range(4):
        for j, (ref, lo, hi) in enumerate(
            ((wq_hbm, 0, FEAT), (wk_hbm, FEAT, FEAT + HEAD), (wv_hbm, FEAT + HEAD, FEAT + 2 * HEAD))
        ):
            loads.append(
                pltpu.make_async_copy(
                    ref.at[pl.ds(i * WIDTH, WIDTH)], w.at[i, :, lo:hi], wsem.at[3 * i + j]
                )
            )
    loads_out = [
        pltpu.make_async_copy(wo_hbm.at[:, pl.ds(i * WIDTH, WIDTH)], wo.at[i], wsem.at[12 + i])
        for i in range(4)
    ]
    for copy in loads + loads_out:
        copy.start()

    barrier = pltpu.get_barrier_semaphore()
    for device in (to_right, to_left, sibling):
        pl.semaphore_signal(barrier, inc=1, device_id=device, device_id_type=MESH)
    for d in range(1, REACH + 1):
        @pl.when(chip + d < CHIPS)
        def _():
            pl.semaphore_signal(
                barrier, inc=1, device_id={"seq": s + 2 * d, "tp": t}, device_id_type=MESH
            )

        @pl.when(chip >= d)
        def _():
            pl.semaphore_signal(
                barrier, inc=1, device_id={"seq": s - 2 * d, "tp": t}, device_id_type=MESH
            )
    pl.semaphore_wait(
        barrier, 3 + jnp.minimum(chip, REACH) + jnp.minimum(CHIPS - 1 - chip, REACH)
    )

    def unit(u):
        src, buf = (tok, tk) if u < 4 else (grad, gr)
        return src, buf, pl.ds((u % 4) * CHUNK, CHUNK)

    def send(u, way):
        src, buf, sl = unit(u)
        if way == 0:
            return remote(src.at[sl], buf.at[0, sl], ys.at[u, 0], yr.at[u, 0], to_right)
        return remote(src.at[sl], buf.at[2, sl], ys.at[u, 1], yr.at[u, 1], to_left)

    def forward(u):
        _, buf, sl = unit(u)
        if u % 2 == 0:
            return remote(buf.at[0, sl], buf.at[1, sl], fs.at[u], fr.at[u], to_right)
        return remote(buf.at[2, sl], buf.at[1, sl], fs.at[u], fr.at[u], to_left)

    def issue(u):
        for way in range(2):
            send(u, way).start()

    def pump(u):
        send(u, u % 2).wait_recv()
        forward(u).start()

    def rest(u):
        send(u, 1 - u % 2).wait_recv()

    def kv_send(d, hf):
        here = kv.at[chip, core, hf]
        return remote(here, here, kvs.at[d - 1, hf], kvr.at[d - 1, hf], {"seq": s + 2 * d, "tp": t})

    def kv_arrival(d, hf):
        there = kv.at[chip - d, core, hf]
        return remote(there, there, kvs.at[d - 1, hf], kvr.at[d - 1, hf], sibling)

    def kv_sibling(d, hf):
        there = kv.at[chip - d, core, hf]
        return remote(there, there, sbs.at[d, hf], sbr.at[d, hf], sibling)

    def make_rows(hf):
        sl = pl.ds(hf * HALF, HALF)
        cos, sin = cos_ref[sl, :], sin_ref[sl, :]

        def rotated(i):
            u = acc[sl, i * HEAD : (i + 1) * HEAD] + bias[:, i * HEAD : (i + 1) * HEAD]
            return (u * cos + pltpu.roll(u, HEAD // 2, 1) * sin).astype(BF16)

        kv[chip, core, hf, :, :HEAD] = rotated(HEADS)
        kv[chip, core, hf, :, HEAD:] = (
            acc[sl, (HEADS + 1) * HEAD :] + bias[:, (HEADS + 1) * HEAD :]
        ).astype(BF16)
        kv_sibling(0, hf).start()
        for d in range(1, REACH + 1):
            @pl.when(chip + d < CHIPS)
            def _():
                kv_send(d, hf).start()
        for h in range(HEADS):
            q = rotated(h)
            qn[h, sl, :] = q
            qt[:, pl.ds(h * ROWS + hf * HALF, HALF)] = q.T

    issue(0)
    issue(1)
    for copy in loads:
        copy.wait()
    acc[...] = nn(tok[...], w[t])
    pump(0)
    issue(2)
    for copy in loads_out:
        copy.wait()
    gacc[...] = nt(grad[...], wo[t])
    m_s[...] = jnp.full(m_s.shape, neg_large, F32)
    l_s[...] = jnp.zeros(l_s.shape, F32)
    oacc[...] = jnp.zeros(oacc.shape, F32)
    pump(1)
    issue(3)
    for hf in range(2):
        sl = pl.ds(hf * HALF, HALF)
        if hf == 1:
            pump(2)
            issue(4)
            pump(3)
            issue(5)
        for u in (2 * hf, 2 * hf + 1):
            rest(u)
        acc[sl, :] += nn(tk[0, sl, :], w[left])
        acc[sl, :] += nn(tk[2, sl, :], w[right])
        for u in (2 * hf, 2 * hf + 1):
            forward(u).wait_recv()
        acc[sl, :] += nn(tk[1, sl, :], w[opp])
        make_rows(hf)

    for hf in range(2):
        for d in range(1, REACH + 1):
            @pl.when(chip >= d)
            def _():
                kv_arrival(d, hf).wait_recv()
                kv_sibling(d, hf).start()

    first_key = start_ref[...]
    row_index = s * ROWS + lax.broadcasted_iota(jnp.int32, (1, ROWS), 1)

    def attend(d):
        both = kv[chip - d].reshape(4 * HALF, 2 * HEAD)
        k = both[:, :HEAD]
        vt = both[:, HEAD:].T
        key = (chip - d) * (4 * HALF) + lax.broadcasted_iota(jnp.int32, (4 * HALF, ROWS), 0)
        allowed = (key >= first_key) & (key <= row_index)
        following = nn(k, qt[:, :ROWS])
        held = None
        for h in range(HEADS + 1):
            sl = slice(h * ROWS, (h + 1) * ROWS)
            raw = following
            if h + 1 < HEADS:
                following = nn(k, qt[:, (h + 1) * ROWS : (h + 2) * ROWS])
            if held is not None:
                cols, weights, shrink = held
                oacc[:, cols] = oacc[:, cols] * shrink + nn(vt, weights)
            if h < HEADS:
                scores = jnp.where(allowed, raw * scale, neg_large)
                old = m_s[:, sl]
                top = jnp.maximum(old, jnp.max(scores, axis=0, keepdims=True))
                weights = jnp.exp2(scores - top)
                shrink = jnp.exp2(old - top)
                l_s[:, sl] = l_s[:, sl] * shrink + jnp.sum(weights, axis=0, keepdims=True)
                m_s[:, sl] = top
                held = (sl, weights.astype(BF16), shrink)

    pump(4)
    issue(6)

    def forward_step(d, carry):
        @pl.when(chip >= d)
        def _():
            for hf in range(2):
                kv_sibling(d, hf).wait_recv()
            attend(d)

        @pl.when(d == 2)
        def _():
            pump(5)
            issue(7)

        @pl.when(d == 6)
        def _():
            pump(6)

        return carry

    lax.fori_loop(0, REACH + 1, forward_step, 0)
    for h in range(HEADS):
        sl = slice(h * ROWS, (h + 1) * ROWS)
        mass = l_s[:, sl]
        o = (oacc[:, sl] / mass).astype(BF16)
        att[:, sl] = o
        at[:, h * HEAD : (h + 1) * HEAD] = o.T
        lse[:, sl] = m_s[:, sl] + jnp.log2(mass)

    def scatter_copy(i, part, arrived, passing, n):
        a, b = pl.ds(0, HALF), pl.ds(HALF, HALF)
        src, dst, device = (
            (part.at[1, a], passing.at[0], to_right),
            (part.at[1, b], passing.at[1], to_left),
            (part.at[2, b], arrived.at[0, b], to_right),
            (part.at[0, a], arrived.at[1, a], to_left),
            (part.at[2, a], arrived.at[0, a], to_right),
            (part.at[0, b], arrived.at[1, b], to_left),
        )[i]
        return remote(src, dst, rss.at[n, i], rsr.at[n, i], device)

    def scatter_early(share, part, arrived, passing, n):
        for i, (slot, rel, hf) in enumerate(((opp, 1, 0), (opp, 1, 1), (right, 2, 1), (left, 0, 0))):
            part[rel, pl.ds(hf * HALF, HALF), :] = share(slot, hf).astype(BF16)
            scatter_copy(i, part, arrived, passing, n).start()

    def scatter_late(share, part, arrived, passing, n):
        for i, (slot, rel, hf) in enumerate(((right, 2, 0), (left, 0, 1))):
            mine = share(slot, hf)
            scatter_copy(i, part, arrived, passing, n).wait_recv()
            part[rel, pl.ds(hf * HALF, HALF), :] = (mine + passing[i].astype(F32)).astype(BF16)
            scatter_copy(4 + i, part, arrived, passing, n).start()

    def scatter_end(share, part, arrived, passing, n, result):
        for hf, waits in ((1, (2, 5)), (0, (3, 4))):
            sl = pl.ds(hf * HALF, HALF)
            mine = share(t, hf)
            for i in waits:
                scatter_copy(i, part, arrived, passing, n).wait_recv()
            result[sl, :] = (
                mine + arrived[0, sl, :].astype(F32) + arrived[1, sl, :].astype(F32)
            ).astype(BF16)
        for i in range(6):
            scatter_copy(i, part, arrived, passing, n).wait_send()

    def out_share(slot, hf):
        return nn(at[pl.ds(hf * HALF, HALF), :], wo[slot])

    pump(7)
    scatter_early(out_share, p_out, v_out, f_out, 0)

    for hf in range(2):
        sl = pl.ds(hf * HALF, HALF)
        for u in (4 + 2 * hf, 5 + 2 * hf):
            rest(u)
            forward(u).wait_recv()
        g = gacc[sl, :] + nt(gr[0, sl, :], wo[left])
        g = g + nt(gr[2, sl, :], wo[right])
        g = (g + nt(gr[1, sl, :], wo[opp])).astype(BF16)
        for h in range(HEADS):
            part = g[:, h * HEAD : (h + 1) * HEAD]
            gn[h, sl, :] = part
            gt[:, pl.ds(h * ROWS + hf * HALF, HALF)] = part.T
    delta[...] = jnp.sum(gt[...].astype(F32) * att[...].astype(F32), axis=0, keepdims=True)
    oacc[...] = jnp.zeros(oacc.shape, F32)

    def dkv_sibling(d, hf):
        return remote(sib_out.at[d, hf], sib_in.at[d, hf], dss.at[d, hf], dsr.at[d, hf], sibling)

    def dkv_send(d, hf):
        return remote(
            dkv_out.at[d - 1, hf], dkv_in.at[d - 1, hf], dos.at[d - 1, hf], dor.at[d - 1, hf],
            {"seq": s - 2 * d, "tp": t},
        )

    def backward(d, hf):
        both = kv[chip - d, :, hf].reshape(2 * HALF, 2 * HEAD)
        k, v = both[:, :HEAD], both[:, HEAD:]
        kt = k.T
        r = lax.broadcasted_iota(jnp.int32, (2 * HALF, ROWS), 0)
        key = (chip - d) * (4 * HALF) + hf * HALF + jnp.where(r >= HALF, r + HALF, r)
        allowed = (key >= first_key) & (key <= row_index)
        following = (nn(k, qt[:, :ROWS]), nn(v, gt[:, :ROWS]))
        held = None
        dk = jnp.zeros((2 * HALF, HEAD), F32)
        dv = jnp.zeros((2 * HALF, HEAD), F32)
        for h in range(HEADS + 1):
            sl = slice(h * ROWS, (h + 1) * ROWS)
            raw, dprob = following
            if h + 1 < HEADS:
                nxt = slice((h + 1) * ROWS, (h + 2) * ROWS)
                following = (nn(k, qt[:, nxt]), nn(v, gt[:, nxt]))
            if held is not None:
                cols, prob_b, ds_b = held
                dv = dv + nn(prob_b, gn[h - 1])
                dk = dk + nn(ds_b, qn[h - 1])
                oacc[:, cols] = oacc[:, cols] + nn(kt, ds_b)
            if h < HEADS:
                prob = jnp.where(allowed, jnp.exp2(raw * scale - lse[:, sl]), 0.0)
                ds = prob * (dprob - delta[:, sl])
                held = (sl, prob.astype(BF16), ds.astype(BF16))
        tmp[:, :, :HEAD] = (dk * factor).reshape(2, HALF, HEAD)
        tmp[:, :, HEAD:] = dv.reshape(2, HALF, HEAD)
        own[d, hf] = tmp[core]
        sib_out[d, hf] = tmp[1 - core].astype(BF16)
        dkv_sibling(d, hf).start()

    def dkv_pump(i):
        d, hf = REACH - lax.div(i, 2), lax.rem(i, 2)

        @pl.when((chip >= d) & (d > 0))
        def _():
            dkv_sibling(d, hf).wait_recv()
            dkv_out[d - 1, hf] = (own[d, hf] + sib_in[d, hf].astype(F32)).astype(BF16)
            dkv_send(d, hf).start()

    def backward_step(i, carry):
        d, hf = REACH - lax.div(i, 2), lax.rem(i, 2)

        @pl.when(chip >= d)
        def _():
            backward(d, hf)

        @pl.when(i > 0)
        def _():
            dkv_pump(i - 1)

        @pl.when(i == 10)
        def _():
            scatter_late(out_share, p_out, v_out, f_out, 0)

        return carry

    lax.fori_loop(0, 2 * (REACH + 1), backward_step, 0)
    for h in range(HEADS):
        u = oacc[:, h * ROWS : (h + 1) * ROWS].T * factor
        x[:, h * HEAD : (h + 1) * HEAD] = (
            u * cos_ref[...] - pltpu.roll(u, HEAD // 2, 1) * sin_ref[...]
        ).astype(BF16)
    for hf in range(2):
        dkv_sibling(0, hf).wait_recv()
        own[0, hf] = own[0, hf] + sib_in[0, hf].astype(F32)
        for d in range(1, REACH + 1):
            @pl.when(chip + d < CHIPS)
            def _():
                dkv_send(d, hf).wait_recv()
                own[0, hf] = own[0, hf] + dkv_in[d - 1, hf].astype(F32)
        sl = pl.ds(hf * HALF, HALF)
        u = own[0, hf, :, :HEAD]
        x[sl, FEAT : FEAT + HEAD] = (
            u * cos_ref[sl, :] - pltpu.roll(u, HEAD // 2, 1) * sin_ref[sl, :]
        ).astype(BF16)
        x[sl, FEAT + HEAD :] = own[0, hf, :, HEAD:].astype(BF16)

    def grad_share(slot, hf):
        return nt(x[pl.ds(hf * HALF, HALF), :], w[slot])

    scatter_early(grad_share, p_grad, v_grad, f_grad, 1)
    scatter_end(out_share, p_out, v_out, f_out, 0, out_ref)
    scatter_late(grad_share, p_grad, v_grad, f_grad, 1)

    for u in range(8):
        for way in range(2):
            send(u, way).wait_send()
        forward(u).wait_send()
    for hf in range(2):
        kv_sibling(0, hf).wait_send()
        dkv_sibling(0, hf).wait_send()
        for d in range(1, REACH + 1):
            @pl.when(chip + d < CHIPS)
            def _():
                kv_send(d, hf).wait_send()

            @pl.when(chip >= d)
            def _():
                kv_sibling(d, hf).wait_send()
                dkv_sibling(d, hf).wait_send()
                dkv_send(d, hf).wait_send()
    scatter_end(grad_share, p_grad, v_grad, f_grad, 1, gtok_ref)


def local(
    tokens, w_query, b_query, w_key, key_bias, value_weight, value_bias, w_out, doc_lengths, grad_out
):
    mine = lax.axis_index("seq")
    doc_ends = jnp.cumsum(doc_lengths)
    doc_starts = doc_ends - doc_lengths
    index = mine * ROWS + jnp.arange(ROWS, dtype=jnp.int32)
    start = start_of(index, doc_starts, doc_ends)
    cos, sin = rope_tables(index - start)
    bias = jnp.concatenate([b_query, key_bias, value_bias]).astype(F32)[None, :]
    vm = pl.BlockSpec(memory_space=pltpu.VMEM)
    hbm = pl.BlockSpec(memory_space=pl.ANY)
    dma = pltpu.SemaphoreType.DMA
    shape = jax.ShapeDtypeStruct((ROWS, WIDTH), BF16)
    return pl.pallas_call(
        block_kernel,
        out_shape=(shape, shape),
        in_specs=[vm, vm, hbm, hbm, hbm, hbm, vm, vm, vm, vm],
        out_specs=(vm, vm),
        scratch_shapes=[
            pltpu.VMEM((4, WIDTH, FEAT + 2 * HEAD), BF16),
            pltpu.VMEM((4, FEAT, WIDTH), BF16),
            pltpu.VMEM((3, ROWS, WIDTH), BF16),
            pltpu.VMEM((3, ROWS, WIDTH), BF16),
            pltpu.VMEM((ROWS, FEAT + 2 * HEAD), F32),
            pltpu.VMEM((ROWS, FEAT), F32),
            pltpu.VMEM((HEADS, ROWS, HEAD), BF16),
            pltpu.VMEM((HEAD, HEADS * ROWS), BF16),
            pltpu.VMEM((HEADS, ROWS, HEAD), BF16),
            pltpu.VMEM((HEAD, HEADS * ROWS), BF16),
            pltpu.VMEM((CHIPS, 2, 2, HALF, 2 * HEAD), BF16),
            pltpu.VMEM((ROWS, FEAT), BF16),
            pltpu.VMEM((HEAD, HEADS * ROWS), BF16),
            pltpu.VMEM((HEAD, HEADS * ROWS), F32),
            pltpu.VMEM((1, HEADS * ROWS), F32),
            pltpu.VMEM((1, HEADS * ROWS), F32),
            pltpu.VMEM((1, HEADS * ROWS), F32),
            pltpu.VMEM((1, HEADS * ROWS), F32),
            pltpu.VMEM((2, HALF, 2 * HEAD), F32),
            pltpu.VMEM((REACH + 1, 2, HALF, 2 * HEAD), F32),
            pltpu.VMEM((REACH + 1, 2, HALF, 2 * HEAD), BF16),
            pltpu.VMEM((REACH + 1, 2, HALF, 2 * HEAD), BF16),
            pltpu.VMEM((REACH, 2, HALF, 2 * HEAD), BF16),
            pltpu.VMEM((REACH, 2, HALF, 2 * HEAD), BF16),
            pltpu.VMEM((ROWS, FEAT + 2 * HEAD), BF16),
            pltpu.VMEM((3, ROWS, WIDTH), BF16),
            pltpu.VMEM((2, ROWS, WIDTH), BF16),
            pltpu.VMEM((2, HALF, WIDTH), BF16),
            pltpu.VMEM((3, ROWS, WIDTH), BF16),
            pltpu.VMEM((2, ROWS, WIDTH), BF16),
            pltpu.VMEM((2, HALF, WIDTH), BF16),
            dma((16,)),
            dma((8, 2)), dma((8, 2)),
            dma((8,)), dma((8,)),
            dma((REACH, 2)), dma((REACH, 2)),
            dma((REACH + 1, 2)), dma((REACH + 1, 2)),
            dma((REACH + 1, 2)), dma((REACH + 1, 2)),
            dma((REACH, 2)), dma((REACH, 2)),
            dma((2, 6)), dma((2, 6)),
        ],
        compiler_params=pltpu.CompilerParams(
            collective_id=0, has_side_effects=True, vmem_limit_bytes=60 << 20
        ),
        name="attention_block",
    )(
        tokens, grad_out, w_query, w_key, value_weight, w_out, bias, cos, sin,
        start[None, :].astype(jnp.int32),
    )


def solution(mesh):
    return jax.shard_map(
        local,
        mesh=mesh,
        in_specs=(
            P("seq", "tp"),
            P(None, "tp"),
            P("tp"),
            P(None, "tp"),
            P("tp"),
            P(None, "tp"),
            P("tp"),
            P("tp", None),
            P(),
            P("seq", "tp"),
        ),
        out_specs=(P("seq", "tp"), P("seq", "tp")),
        check_vma=False,
    )
```

time: 353 us -> 130 us (0.37)
  waiting for transfers between devices: 269 us -> 0 us
  Pallas kernels: 18.5 us -> 118 us
  matrix products: 35.4 us -> 0 us
  between operations: 16.8 us -> 0.66 us
    reduce_scatter x3 -> x0, waiting for transfers between devices: 169 us -> none  [the longest x1 102 us: local(): lax.psum_scatter(pair_grads, 'seq', scatter_dimension=0, tiled=False)]
    pallas_call x2 -> x1, Pallas kernels: 18.5 us -> 118 us  [local(): pl.pallas_call(block_kernel, out_shape=(shape, shape), in_specs=[vm, vm,...]
    all_gather x3 -> x0, waiting for transfers between devices: 98.7 us -> none  [the longest x1 42.1 us: local(): pairs = lax.all_gather(pair, 'seq', axis=0, tiled=False)]
    dot_general x8 -> x0, matrix products: 35.4 us -> none  [the longest x4 19.2 us: nt(): lax.dot_general(a, b, (((1,), (1,)), ((), ())), preferred_element_type=F32)]
  transfers between devices with their start and end apart: 6 -> 0, of which waited for: 6 -> 0; matrix products, arithmetic and copies ran while one was open for 12% -> 0% of each run, Pallas kernels for 0% -> 0%
where the time goes in v2:
time: 130 us; the launch traced here: 128 us
  Pallas kernels  118 us (91%)
  local copies, waits for them, and re-layouts  4.62 us (4%)
  other arithmetic  4.23 us (3%)
    pallas_call x1, Pallas kernels, local(): pl.pallas_call(block_kernel, out_shape=(shape, shape), in_specs=[vm, vm,...  118 us
    unnamed x4, local copies, waits for them, and re-layouts  3.93 us

profile of v2, /device:TPU:64, one launch (start us, length us, event | category | flops | bytes accessed | tf_op | source)
XLA Modules:
  0.0 127.5 jit_solution(2182739887259676540)
XLA Ops:
  0.6 0.8 reduce-window.8
  1.5 0.7 bitcast_subtract_fusion
  2.1 0.1 select_reduce_fusion
  2.2 0.0 copy-start
  2.2 0.7 concatenate.22
  2.9 1.3 maximum_convert_fusion.bias
  4.2 0.5 fusion
  4.7 0.8 pad_maximum_fusion
  5.6 0.0 copy-done
  5.6 118.0 %attention_block.1 = (bf16[256,1280]{1,0:T(8,128)(2,1)}, bf16[256,1280]{1,0:T(8,128)(2,1)}) custom-call(bf16[256,1280]{1,0:T(8,128)(2,1)} %tok.1, bf16[256,1280]{1,0:T(8,128)(2,1)} %grad.1, bf16[5120,640]{1,0:T(8,128)(2,1)} %wq_hbm.1, bf16[5120,128]{1,0:T(8,128)(2,1)} %wk_hbm.1, bf16[5120,128]{1,0:T(8,128)(2,1)} %wv_hbm.1, bf16[640,5120]{1,0:T(8,128)(2,1)} %wo_hbm.1, ...), custom_call_target="tpu_custom_call" | custom-call | tf_op jit(solution)/shard_map/attention_block/pallas_call | solution.py:452
  123.6 2.0 %copy.14 = bf16[256,1280]{1,0:T(8,128)(2,1)} copy(bf16[256,1280]{1,0:T(8,128)(2,1)} %get-tuple-element.9) | data formatting | bytes 1310720
  125.6 2.0 %copy.15 = bf16[256,1280]{1,0:T(8,128)(2,1)} copy(bf16[256,1280]{1,0:T(8,128)(2,1)} %get-tuple-element.10) | data formatting | bytes 1310720
  (3 shorter events, 0.0 us)
Async XLA Ops:
  2.2 3.3 %copy-start = (s32[256]{0:T(256)}, s32[256]{0:T(256)S(1)}, u32[]{:S(2)}) copy-start(s32[256]{0:T(256)S(1)} %select_reduce_fusion) | copy-start | bytes 3076

commit v3 on v2

--- a/solution.py
+++ b/solution.py
@@ -2,6 +2,7 @@
 
 import jax
 import jax.numpy as jnp
+import numpy as np
 from jax import lax
 from jax.experimental import pallas as pl
 from jax.experimental.pallas import tpu as pltpu
@@ -26,21 +27,6 @@
 scale = factor * log2e
 
 
-def start_of(token_index, doc_starts, doc_ends):
-    inside = (token_index[:, None] >= doc_starts[None, :]) & (
-        token_index[:, None] < doc_ends[None, :]
-    )
-    return jnp.sum(jnp.where(inside, doc_starts[None, :], 0), axis=1)
-
-
-def rope_tables(position):
-    half = HEAD // 2
-    frequency = theta_base ** (-2.0 * jnp.arange(half, dtype=F32) / HEAD)
-    angles = position.astype(F32)[:, None] * frequency[None, :]
-    cos, sin = jnp.cos(angles), jnp.sin(angles)
-    return jnp.concatenate([cos, cos], axis=1), jnp.concatenate([-sin, sin], axis=1)
-
-
 def nn(a, b):
     return lax.dot_general(a, b, (((1,), (0,)), ((), ())), preferred_element_type=F32)
 
@@ -50,9 +36,9 @@
 
 
 def block_kernel(
-    tok, grad, wq_hbm, wk_hbm, wv_hbm, wo_hbm, bias, cos_ref, sin_ref, start_ref,
+    lengths, tok, grad, wq_hbm, wk_hbm, wv_hbm, wo_hbm, bq, bk, bv, freq_ref,
     out_ref, gtok_ref,
-    w, wo, tk, gr, acc, gacc, qn, qt, gn, gt, kv, at, att, oacc, m_s, l_s, lse, delta,
+    cos_ref, sin_ref, w, wo, tk, gr, acc, gacc, qn, qt, gn, gt, kv, at, att, oacc, m_s, l_s, lse, delta,
     tmp, own, sib_out, sib_in, dkv_out, dkv_in, x, p_out, v_out, f_out, p_grad, v_grad, f_grad,
     wsem, ys, yr, fs, fr, kvs, kvr, sbs, sbr, dss, dsr, dos, dor, rss, rsr,
 ):
@@ -62,6 +48,18 @@
     right, left, opp = lax.rem(t + 1, 4), lax.rem(t + 3, 4), lax.rem(t + 2, 4)
     to_right, to_left = {"seq": s, "tp": right}, {"seq": s, "tp": left}
     sibling = {"seq": s + 1 - 2 * core, "tp": t}
+    at_z, at_x = lax.div(chip, 4), lax.rem(chip, 4)
+    m1 = at_x + core * (at_z - at_x)
+    m2 = at_z + core * (at_x - at_z)
+    stride1, stride2 = 1 + 3 * core, 4 - 3 * core
+
+    def place(r2, r1):
+        return lax.rem(m1 + 4 - r1, 4) * stride1 + lax.rem(m2 + 4 - r2, 4) * stride2
+
+    def towards(step2, step1):
+        return {"seq": 2 * place(-step2, -step1) + core, "tp": t}
+
+    up1, down1, up2, down2 = towards(0, 1), towards(0, -1), towards(1, 0), towards(-1, 0)
 
     def remote(src, dst, send, recv, device):
         return pltpu.make_async_remote_copy(
@@ -87,7 +85,8 @@
         copy.start()
 
     barrier = pltpu.get_barrier_semaphore()
-    for device in (to_right, to_left, sibling):
+    partners = (to_right, to_left, sibling, up1, down1, up2, down2)
+    for device in partners:
         pl.semaphore_signal(barrier, inc=1, device_id=device, device_id_type=MESH)
     for d in range(1, REACH + 1):
         @pl.when(chip + d < CHIPS)
@@ -102,7 +101,8 @@
                 barrier, inc=1, device_id={"seq": s - 2 * d, "tp": t}, device_id_type=MESH
             )
     pl.semaphore_wait(
-        barrier, 3 + jnp.minimum(chip, REACH) + jnp.minimum(CHIPS - 1 - chip, REACH)
+        barrier,
+        len(partners) + jnp.minimum(chip, REACH) + jnp.minimum(CHIPS - 1 - chip, REACH),
     )
 
     def unit(u):
@@ -132,13 +132,52 @@
     def rest(u):
         send(u, 1 - u % 2).wait_recv()
 
-    def kv_send(d, hf):
-        here = kv.at[chip, core, hf]
-        return remote(here, here, kvs.at[d - 1, hf], kvr.at[d - 1, hf], {"seq": s + 2 * d, "tp": t})
-
-    def kv_arrival(d, hf):
-        there = kv.at[chip - d, core, hf]
-        return remote(there, there, kvs.at[d - 1, hf], kvr.at[d - 1, hf], sibling)
+    def kv_copy(hf, r2, r1):
+        if r2 == 0:
+            src = (0, 0) if r1 != 2 else (0, 1 + 2 * hf)
+            device = up1 if r1 == 1 or (r1 == 2 and hf == 0) else down1
+        elif r2 == 2:
+            src, device = ((1, r1), up2) if r1 < 2 else ((3, r1), down2)
+        else:
+            src, device = (0, r1), up2 if r2 == 1 else down2
+        here = kv.at[place(*src), core, hf]
+        return remote(here, here, kvs.at[hf, r2, r1], kvr.at[hf, r2, r1], device)
+
+    def kv_start(hf, *slots):
+        for slot in slots:
+            kv_copy(hf, *slot).start()
+
+    def kv_wait(hf, *slots):
+        for r2, r1 in slots:
+            there = kv.at[place(r2, r1), core, hf]
+            remote(there, there, kvs.at[hf, r2, r1], kvr.at[hf, r2, r1], sibling).wait_recv()
+
+    def kv_second(hf):
+        kv_wait(hf, (0, 1))
+        kv_start(hf, *(((0, 2),) if hf == 0 else ()), (1, 1), (3, 1))
+        kv_wait(hf, (0, 3))
+        kv_start(hf, *(((0, 2),) if hf == 1 else ()), (1, 3), (3, 3))
+        kv_wait(hf, (1, 0))
+        kv_start(hf, (2, 0))
+
+    def kv_third(hf):
+        kv_wait(hf, (0, 2))
+        kv_start(hf, (1, 2), (3, 2))
+        kv_wait(hf, (1, 1))
+        kv_start(hf, (2, 1))
+
+    def kv_fourth(hf):
+        kv_wait(hf, (3, 3))
+        kv_start(hf, (2, 3))
+        kv_wait(hf, (3, 2))
+        kv_start(hf, (2, 2))
+
+    def kv_fifth(hf):
+        kv_wait(hf, (1, 2), (1, 3), (3, 0), (3, 1), (2, 0), (2, 1), (2, 2), (2, 3))
+        for d in range(1, REACH + 1):
+            @pl.when(chip >= d)
+            def _():
+                kv_sibling(d, hf).start()
 
     def kv_sibling(d, hf):
         there = kv.at[chip - d, core, hf]
@@ -149,18 +188,16 @@
         cos, sin = cos_ref[sl, :], sin_ref[sl, :]
 
         def rotated(i):
-            u = acc[sl, i * HEAD : (i + 1) * HEAD] + bias[:, i * HEAD : (i + 1) * HEAD]
+            u = acc[sl, i * HEAD : (i + 1) * HEAD]
+            u = u + (bq[:, i * HEAD : (i + 1) * HEAD] if i < HEADS else bk[...]).astype(F32)
             return (u * cos + pltpu.roll(u, HEAD // 2, 1) * sin).astype(BF16)
 
         kv[chip, core, hf, :, :HEAD] = rotated(HEADS)
         kv[chip, core, hf, :, HEAD:] = (
-            acc[sl, (HEADS + 1) * HEAD :] + bias[:, (HEADS + 1) * HEAD :]
+            acc[sl, (HEADS + 1) * HEAD :] + bv[...].astype(F32)
         ).astype(BF16)
+        kv_start(hf, (0, 1), (0, 3), (1, 0), (3, 0))
         kv_sibling(0, hf).start()
-        for d in range(1, REACH + 1):
-            @pl.when(chip + d < CHIPS)
-            def _():
-                kv_send(d, hf).start()
         for h in range(HEADS):
             q = rotated(h)
             qn[h, sl, :] = q
@@ -168,6 +205,23 @@
 
     issue(0)
     issue(1)
+    end0 = lengths[0]
+    end1 = end0 + lengths[1]
+    end2 = end1 + lengths[2]
+
+    def start_at(index):
+        later = jnp.where(index >= end2, end2, jnp.where(index >= end1, end1, end0))
+        return jnp.where(index >= end0, later, 0)
+
+    row_index = s * ROWS + lax.broadcasted_iota(jnp.int32, (1, ROWS), 1)
+    first_key = start_at(row_index)
+    index = s * ROWS + lax.broadcasted_iota(jnp.int32, (ROWS, HEAD), 0)
+    angles = (index - start_at(index)).astype(F32) * freq_ref[...]
+    cos_ref[...] = jnp.cos(angles)
+    sine = jnp.sin(angles)
+    lane = lax.broadcasted_iota(jnp.int32, (ROWS, HEAD), 1)
+    sin_ref[...] = jnp.where(lane < HEAD // 2, -sine, sine)
+
     for copy in loads:
         copy.wait()
     acc[...] = nn(tok[...], w[t])
@@ -192,26 +246,26 @@
             rest(u)
         acc[sl, :] += nn(tk[0, sl, :], w[left])
         acc[sl, :] += nn(tk[2, sl, :], w[right])
+        if hf == 1:
+            kv_second(0)
         for u in (2 * hf, 2 * hf + 1):
             forward(u).wait_recv()
         acc[sl, :] += nn(tk[1, sl, :], w[opp])
         make_rows(hf)
 
-    for hf in range(2):
-        for d in range(1, REACH + 1):
-            @pl.when(chip >= d)
-            def _():
-                kv_arrival(d, hf).wait_recv()
-                kv_sibling(d, hf).start()
-
-    first_key = start_ref[...]
-    row_index = s * ROWS + lax.broadcasted_iota(jnp.int32, (1, ROWS), 1)
-
-    def attend(d):
-        both = kv[chip - d].reshape(4 * HALF, 2 * HEAD)
+    r2 = lax.broadcasted_iota(jnp.int32, (2 * HALF, ROWS), 0)
+    key_at = jnp.where(r2 >= HALF, r2 + HALF, r2)
+
+    def attend(first, second):
+        both = jnp.concatenate(
+            [kv[jnp.maximum(c, 0), :, hf].reshape(2 * HALF, 2 * HEAD) for c, hf in (first, second)],
+            axis=0,
+        )
         k = both[:, :HEAD]
         vt = both[:, HEAD:].T
-        key = (chip - d) * (4 * HALF) + lax.broadcasted_iota(jnp.int32, (4 * HALF, ROWS), 0)
+        key = jnp.concatenate(
+            [key_at + (c * (4 * HALF) + hf * HALF) for c, hf in (first, second)], axis=0
+        )
         allowed = (key >= first_key) & (key <= row_index)
         following = nn(k, qt[:, :ROWS])
         held = None
@@ -233,28 +287,54 @@
                 m_s[:, sl] = top
                 held = (sl, weights.astype(BF16), shrink)
 
-    pump(4)
+    def forward_step(i, carry):
+        j, hf = lax.rem(i + 3, 4), lax.div(i + 3, 4) - 1
+        d = 2 * j + 1
+        is_own = i == 0
+
+        @pl.when(i == 1)
+        def _():
+            kv_third(1)
+            pump(4)
+            kv_fourth(1)
+            kv_fifth(0)
+
+        @pl.when(i == 3)
+        def _():
+            pump(5)
+            kv_fifth(1)
+
+        @pl.when(i == 5)
+        def _():
+            pump(6)
+            pump(7)
+
+        for e in range(2):
+            @pl.when((i > 0) & (chip >= d + e))
+            def _():
+                kv_sibling(d + e, hf).wait_recv()
+
+        @pl.when(is_own | (chip >= d))
+        def _():
+            attend(
+                (jnp.where(is_own, chip, chip - d), jnp.where(is_own, 0, hf)),
+                (jnp.where(is_own, chip, chip - d - 1), jnp.where(is_own, 1, hf)),
+            )
+
+        return carry
+
     issue(6)
-
-    def forward_step(d, carry):
-        @pl.when(chip >= d)
-        def _():
-            for hf in range(2):
-                kv_sibling(d, hf).wait_recv()
-            attend(d)
-
-        @pl.when(d == 2)
-        def _():
-            pump(5)
-            issue(7)
-
-        @pl.when(d == 6)
-        def _():
-            pump(6)
-
-        return carry
-
+    issue(7)
+    kv_third(0)
+    kv_fourth(0)
+    kv_second(1)
+    for hf in range(2):
+        kv_sibling(0, hf).wait_recv()
     lax.fori_loop(0, REACH + 1, forward_step, 0)
+    for u in range(4, 8):
+        rest(u)
+    gacc[...] += nt(gr[0], wo[left])
+    gacc[...] += nt(gr[2], wo[right])
     for h in range(HEADS):
         sl = slice(h * ROWS, (h + 1) * ROWS)
         mass = l_s[:, sl]
@@ -263,11 +343,20 @@
         at[:, h * HEAD : (h + 1) * HEAD] = o.T
         lse[:, sl] = m_s[:, sl] + jnp.log2(mass)
 
+    def pieces(n):
+        return ((0, HALF), (HALF, HALF)) if n == 0 else (
+            ((n - 1) * HALF, CHUNK), ((n - 1) * HALF + CHUNK, CHUNK)
+        )
+
+    def passing_rows(n):
+        return pl.ds(0, HALF) if n == 0 else pl.ds((n - 1) * CHUNK, CHUNK)
+
     def scatter_copy(i, part, arrived, passing, n):
-        a, b = pl.ds(0, HALF), pl.ds(HALF, HALF)
+        a, b = [pl.ds(*piece) for piece in pieces(n)]
+        over = passing_rows(n)
         src, dst, device = (
-            (part.at[1, a], passing.at[0], to_right),
-            (part.at[1, b], passing.at[1], to_left),
+            (part.at[1, a], passing.at[0, over], to_right),
+            (part.at[1, b], passing.at[1, over], to_left),
             (part.at[2, b], arrived.at[0, b], to_right),
             (part.at[0, a], arrived.at[1, a], to_left),
             (part.at[2, a], arrived.at[0, a], to_right),
@@ -276,21 +365,23 @@
         return remote(src, dst, rss.at[n, i], rsr.at[n, i], device)
 
     def scatter_early(share, part, arrived, passing, n):
-        for i, (slot, rel, hf) in enumerate(((opp, 1, 0), (opp, 1, 1), (right, 2, 1), (left, 0, 0))):
-            part[rel, pl.ds(hf * HALF, HALF), :] = share(slot, hf).astype(BF16)
+        for i, (slot, rel, e) in enumerate(((opp, 1, 0), (opp, 1, 1), (right, 2, 1), (left, 0, 0))):
+            sl = pl.ds(*pieces(n)[e])
+            part[rel, sl, :] = share(slot, sl).astype(BF16)
             scatter_copy(i, part, arrived, passing, n).start()
 
     def scatter_late(share, part, arrived, passing, n):
-        for i, (slot, rel, hf) in enumerate(((right, 2, 0), (left, 0, 1))):
-            mine = share(slot, hf)
+        for i, (slot, rel, e) in enumerate(((right, 2, 0), (left, 0, 1))):
+            sl = pl.ds(*pieces(n)[e])
+            mine = share(slot, sl)
             scatter_copy(i, part, arrived, passing, n).wait_recv()
-            part[rel, pl.ds(hf * HALF, HALF), :] = (mine + passing[i].astype(F32)).astype(BF16)
+            part[rel, sl, :] = (mine + passing[i, passing_rows(n), :].astype(F32)).astype(BF16)
             scatter_copy(4 + i, part, arrived, passing, n).start()
 
     def scatter_end(share, part, arrived, passing, n, result):
-        for hf, waits in ((1, (2, 5)), (0, (3, 4))):
-            sl = pl.ds(hf * HALF, HALF)
-            mine = share(t, hf)
+        for e, waits in ((1, (2, 5)), (0, (3, 4))):
+            sl = pl.ds(*pieces(n)[e])
+            mine = share(t, sl)
             for i in waits:
                 scatter_copy(i, part, arrived, passing, n).wait_recv()
             result[sl, :] = (
@@ -299,20 +390,16 @@
         for i in range(6):
             scatter_copy(i, part, arrived, passing, n).wait_send()
 
-    def out_share(slot, hf):
-        return nn(at[pl.ds(hf * HALF, HALF), :], wo[slot])
-
-    pump(7)
+    def out_share(slot, sl):
+        return nn(at[sl, :], wo[slot])
+
     scatter_early(out_share, p_out, v_out, f_out, 0)
 
     for hf in range(2):
         sl = pl.ds(hf * HALF, HALF)
         for u in (4 + 2 * hf, 5 + 2 * hf):
-            rest(u)
             forward(u).wait_recv()
-        g = gacc[sl, :] + nt(gr[0, sl, :], wo[left])
-        g = g + nt(gr[2, sl, :], wo[right])
-        g = (g + nt(gr[1, sl, :], wo[opp])).astype(BF16)
+        g = (gacc[sl, :] + nt(gr[1, sl, :], wo[opp])).astype(BF16)
         for h in range(HEADS):
             part = g[:, h * HEAD : (h + 1) * HEAD]
             gn[h, sl, :] = part
@@ -333,8 +420,7 @@
         both = kv[chip - d, :, hf].reshape(2 * HALF, 2 * HEAD)
         k, v = both[:, :HEAD], both[:, HEAD:]
         kt = k.T
-        r = lax.broadcasted_iota(jnp.int32, (2 * HALF, ROWS), 0)
-        key = (chip - d) * (4 * HALF) + hf * HALF + jnp.where(r >= HALF, r + HALF, r)
+        key = key_at + ((chip - d) * (4 * HALF) + hf * HALF)
         allowed = (key >= first_key) & (key <= row_index)
         following = (nn(k, qt[:, :ROWS]), nn(v, gt[:, :ROWS]))
         held = None
@@ -361,8 +447,10 @@
         sib_out[d, hf] = tmp[1 - core].astype(BF16)
         dkv_sibling(d, hf).start()
 
+    span = REACH + 1
+
     def dkv_pump(i):
-        d, hf = REACH - lax.div(i, 2), lax.rem(i, 2)
+        d, hf = REACH - lax.rem(i, span), lax.div(i, span)
 
         @pl.when((chip >= d) & (d > 0))
         def _():
@@ -371,7 +459,7 @@
             dkv_send(d, hf).start()
 
     def backward_step(i, carry):
-        d, hf = REACH - lax.div(i, 2), lax.rem(i, 2)
+        d, hf = REACH - lax.rem(i, span), lax.div(i, span)
 
         @pl.when(chip >= d)
         def _():
@@ -381,19 +469,19 @@
         def _():
             dkv_pump(i - 1)
 
-        @pl.when(i == 10)
+        @pl.when(i == span - 1)
         def _():
             scatter_late(out_share, p_out, v_out, f_out, 0)
 
         return carry
 
-    lax.fori_loop(0, 2 * (REACH + 1), backward_step, 0)
+    lax.fori_loop(0, 2 * span, backward_step, 0)
     for h in range(HEADS):
         u = oacc[:, h * ROWS : (h + 1) * ROWS].T * factor
         x[:, h * HEAD : (h + 1) * HEAD] = (
             u * cos_ref[...] - pltpu.roll(u, HEAD // 2, 1) * sin_ref[...]
         ).astype(BF16)
-    for hf in range(2):
+    def finish_pair(hf):
         dkv_sibling(0, hf).wait_recv()
         own[0, hf] = own[0, hf] + sib_in[0, hf].astype(F32)
         for d in range(1, REACH + 1):
@@ -408,53 +496,52 @@
         ).astype(BF16)
         x[sl, FEAT + HEAD :] = own[0, hf, :, HEAD:].astype(BF16)
 
-    def grad_share(slot, hf):
-        return nt(x[pl.ds(hf * HALF, HALF), :], w[slot])
-
+    def grad_share(slot, sl):
+        return nt(x[sl, :], w[slot])
+
+    finish_pair(0)
     scatter_early(grad_share, p_grad, v_grad, f_grad, 1)
     scatter_end(out_share, p_out, v_out, f_out, 0, out_ref)
     scatter_late(grad_share, p_grad, v_grad, f_grad, 1)
+    finish_pair(1)
+    scatter_early(grad_share, p_grad, v_grad, f_grad, 2)
+    scatter_end(grad_share, p_grad, v_grad, f_grad, 1, gtok_ref)
+    scatter_late(grad_share, p_grad, v_grad, f_grad, 2)
 
     for u in range(8):
         for way in range(2):
             send(u, way).wait_send()
         forward(u).wait_send()
     for hf in range(2):
-        kv_sibling(0, hf).wait_send()
-        dkv_sibling(0, hf).wait_send()
-        for d in range(1, REACH + 1):
-            @pl.when(chip + d < CHIPS)
-            def _():
-                kv_send(d, hf).wait_send()
-
+        for j in range(1, 16):
+            kv_copy(hf, j // 4, j % 4).wait_send()
+        for d in range(REACH + 1):
             @pl.when(chip >= d)
             def _():
                 kv_sibling(d, hf).wait_send()
                 dkv_sibling(d, hf).wait_send()
-                dkv_send(d, hf).wait_send()
-    scatter_end(grad_share, p_grad, v_grad, f_grad, 1, gtok_ref)
+                if d > 0:
+                    dkv_send(d, hf).wait_send()
+    scatter_end(grad_share, p_grad, v_grad, f_grad, 2, gtok_ref)
 
 
 def local(
     tokens, w_query, b_query, w_key, key_bias, value_weight, value_bias, w_out, doc_lengths, grad_out
 ):
-    mine = lax.axis_index("seq")
-    doc_ends = jnp.cumsum(doc_lengths)
-    doc_starts = doc_ends - doc_lengths
-    index = mine * ROWS + jnp.arange(ROWS, dtype=jnp.int32)
-    start = start_of(index, doc_starts, doc_ends)
-    cos, sin = rope_tables(index - start)
-    bias = jnp.concatenate([b_query, key_bias, value_bias]).astype(F32)[None, :]
+    freq = theta_base ** (-2.0 * np.arange(HEAD // 2) / HEAD)
+    freq = jnp.asarray(np.concatenate([freq, freq])[None, :], F32)
     vm = pl.BlockSpec(memory_space=pltpu.VMEM)
     hbm = pl.BlockSpec(memory_space=pl.ANY)
     dma = pltpu.SemaphoreType.DMA
     shape = jax.ShapeDtypeStruct((ROWS, WIDTH), BF16)
-    return pl.pallas_call(
+    results = pl.pallas_call(
         block_kernel,
         out_shape=(shape, shape),
-        in_specs=[vm, vm, hbm, hbm, hbm, hbm, vm, vm, vm, vm],
+        in_specs=[pl.BlockSpec(memory_space=pltpu.SMEM), vm, vm, hbm, hbm, hbm, hbm, vm, vm, vm, vm],
         out_specs=(vm, vm),
         scratch_shapes=[
+            pltpu.VMEM((ROWS, HEAD), F32),
+            pltpu.VMEM((ROWS, HEAD), F32),
             pltpu.VMEM((4, WIDTH, FEAT + 2 * HEAD), BF16),
             pltpu.VMEM((4, FEAT, WIDTH), BF16),
             pltpu.VMEM((3, ROWS, WIDTH), BF16),
@@ -489,20 +576,21 @@
             dma((16,)),
             dma((8, 2)), dma((8, 2)),
             dma((8,)), dma((8,)),
-            dma((REACH, 2)), dma((REACH, 2)),
+            dma((2, 4, 4)), dma((2, 4, 4)),
             dma((REACH + 1, 2)), dma((REACH + 1, 2)),
             dma((REACH + 1, 2)), dma((REACH + 1, 2)),
             dma((REACH, 2)), dma((REACH, 2)),
-            dma((2, 6)), dma((2, 6)),
+            dma((3, 6)), dma((3, 6)),
         ],
         compiler_params=pltpu.CompilerParams(
             collective_id=0, has_side_effects=True, vmem_limit_bytes=60 << 20
         ),
         name="attention_block",
     )(
-        tokens, grad_out, w_query, w_key, value_weight, w_out, bias, cos, sin,
-        start[None, :].astype(jnp.int32),
+        doc_lengths, tokens, grad_out, w_query, w_key, value_weight, w_out,
+        b_query[None, :], key_bias[None, :], value_bias[None, :], freq,
     )
+    return results
 
 
 def solution(mesh):

time: 130 us -> 119 us (0.915); the launches traced: 128 us -> 119 us
  Pallas kernels: 118 us -> 113 us
  other arithmetic: 4.23 us -> 0 us
    pallas_call x1, Pallas kernels: 118 us -> 113 us  [local(): pl.pallas_call(block_kernel, out_shape=(shape, shape), in_specs=[pl.Block...]
    unnamed x4 -> x2, local copies, waits for them, and re-layouts: 3.93 us -> 3.93 us
where the time goes in v3:
time: 119 us
  Pallas kernels  113 us (95%)
  local copies, waits for them, and re-layouts  5.19 us (4%)
    pallas_call x1, Pallas kernels, local(): pl.pallas_call(block_kernel, out_shape=(shape, shape), in_specs=[pl.Block...  113 us
    unnamed x2, local copies, waits for them, and re-layouts  3.93 us

profile of v3, /device:TPU:64, one launch (start us, length us, event | category | flops | bytes accessed | tf_op | source)
XLA Modules:
  0.0 118.5 jit_solution(9417298416848466107)
XLA Ops:
  0.6 1.3 %broadcast_in_dim.9.bq = bf16[1,640]{1,0:T(2,128)(2,1)} reshape(bf16[640]{0:T(1024)(128)(2,1)} %param.13) | data formatting | bytes 2560 | tf_op jit(solution)/shard_map/broadcast_in_dim | solution.py:591
  1.9 112.7 %attention_block.1 = (bf16[256,1280]{1,0:T(8,128)(2,1)}, bf16[256,1280]{1,0:T(8,128)(2,1)}) custom-call(s32[4]{0:T(128)} %lengths.1, bf16[256,1280]{1,0:T(8,128)(2,1)} %tok.1, bf16[256,1280]{1,0:T(8,128)(2,1)} %grad.1, bf16[5120,640]{1,0:T(8,128)(2,1)} %wq_hbm.1, bf16[5120,128]{1,0:T(8,128)(2,1)} %wk_hbm.1, bf16[5120,128]{1,0:T(8,128)(2,1)} %wv_hbm.1, ...), custom_call_target="tpu_custom_call" | custom-call | tf_op jit(solution)/shard_map/attention_block/pallas_call | solution.py:537
  114.6 2.0 %copy.15 = bf16[256,1280]{1,0:T(8,128)(2,1)} copy(bf16[256,1280]{1,0:T(8,128)(2,1)} %get-tuple-element.4) | data formatting | bytes 1310720
  116.6 2.0 %copy.16 = bf16[256,1280]{1,0:T(8,128)(2,1)} copy(bf16[256,1280]{1,0:T(8,128)(2,1)} %get-tuple-element.5) | data formatting | bytes 1310720

commit v4 on v3

--- a/solution.py
+++ b/solution.py
@@ -39,7 +39,7 @@
     lengths, tok, grad, wq_hbm, wk_hbm, wv_hbm, wo_hbm, bq, bk, bv, freq_ref,
     out_ref, gtok_ref,
     cos_ref, sin_ref, w, wo, tk, gr, acc, gacc, qn, qt, gn, gt, kv, at, att, oacc, m_s, l_s, lse, delta,
-    tmp, own, sib_out, sib_in, dkv_out, dkv_in, x, p_out, v_out, f_out, p_grad, v_grad, f_grad,
+    tmp, own, sib_out, sib_in, dkv_out, dkv_in, x, p_out, v_out, f_out, p_grad, v_grad, f_grad, kept,
     wsem, ys, yr, fs, fr, kvs, kvr, sbs, sbr, dss, dsr, dos, dor, rss, rsr,
 ):
     s = lax.axis_index("seq")
@@ -60,6 +60,7 @@
         return {"seq": 2 * place(-step2, -step1) + core, "tp": t}
 
     up1, down1, up2, down2 = towards(0, 1), towards(0, -1), towards(1, 0), towards(-1, 0)
+    across1 = towards(0, 2)
 
     def remote(src, dst, send, recv, device):
         return pltpu.make_async_remote_copy(
@@ -85,7 +86,7 @@
         copy.start()
 
     barrier = pltpu.get_barrier_semaphore()
-    partners = (to_right, to_left, sibling, up1, down1, up2, down2)
+    partners = (to_right, to_left, sibling, up1, down1, up2, down2, across1)
     for device in partners:
         pl.semaphore_signal(barrier, inc=1, device_id=device, device_id_type=MESH)
     for d in range(1, REACH + 1):
@@ -115,27 +116,31 @@
             return remote(src.at[sl], buf.at[0, sl], ys.at[u, 0], yr.at[u, 0], to_right)
         return remote(src.at[sl], buf.at[2, sl], ys.at[u, 1], yr.at[u, 1], to_left)
 
-    def forward(u):
-        _, buf, sl = unit(u)
-        if u % 2 == 0:
-            return remote(buf.at[0, sl], buf.at[1, sl], fs.at[u], fr.at[u], to_right)
-        return remote(buf.at[2, sl], buf.at[1, sl], fs.at[u], fr.at[u], to_left)
+    def forward(u, way):
+        _, buf, _ = unit(u)
+        sl = pl.ds((u % 4) * CHUNK + way * (CHUNK // 2), CHUNK // 2)
+        return remote(
+            buf.at[2 * way, sl], buf.at[1, sl], fs.at[u, way], fr.at[u, way],
+            to_left if way else to_right,
+        )
 
     def issue(u):
         for way in range(2):
             send(u, way).start()
 
     def pump(u):
-        send(u, u % 2).wait_recv()
-        forward(u).start()
-
-    def rest(u):
-        send(u, 1 - u % 2).wait_recv()
+        for way in range(2):
+            send(u, way).wait_recv()
+            forward(u, way).start()
+
+    def passed(u):
+        for way in range(2):
+            forward(u, way).wait_recv()
 
     def kv_copy(hf, r2, r1):
         if r2 == 0:
-            src = (0, 0) if r1 != 2 else (0, 1 + 2 * hf)
-            device = up1 if r1 == 1 or (r1 == 2 and hf == 0) else down1
+            src = (0, 0)
+            device = (up1, across1, down1)[r1 - 1]
         elif r2 == 2:
             src, device = ((1, r1), up2) if r1 < 2 else ((3, r1), down2)
         else:
@@ -153,20 +158,15 @@
             remote(there, there, kvs.at[hf, r2, r1], kvr.at[hf, r2, r1], sibling).wait_recv()
 
     def kv_second(hf):
-        kv_wait(hf, (0, 1))
-        kv_start(hf, *(((0, 2),) if hf == 0 else ()), (1, 1), (3, 1))
-        kv_wait(hf, (0, 3))
-        kv_start(hf, *(((0, 2),) if hf == 1 else ()), (1, 3), (3, 3))
         kv_wait(hf, (1, 0))
         kv_start(hf, (2, 0))
+        for r1 in (1, 3, 2):
+            kv_wait(hf, (0, r1))
+            kv_start(hf, (1, r1), (3, r1))
 
     def kv_third(hf):
-        kv_wait(hf, (0, 2))
-        kv_start(hf, (1, 2), (3, 2))
         kv_wait(hf, (1, 1))
         kv_start(hf, (2, 1))
-
-    def kv_fourth(hf):
         kv_wait(hf, (3, 3))
         kv_start(hf, (2, 3))
         kv_wait(hf, (3, 2))
@@ -189,22 +189,22 @@
 
         def rotated(i):
             u = acc[sl, i * HEAD : (i + 1) * HEAD]
-            u = u + (bq[:, i * HEAD : (i + 1) * HEAD] if i < HEADS else bk[...]).astype(F32)
+            u = u + (bq[i * HEAD : (i + 1) * HEAD] if i < HEADS else bk[...]).astype(F32)
             return (u * cos + pltpu.roll(u, HEAD // 2, 1) * sin).astype(BF16)
 
         kv[chip, core, hf, :, :HEAD] = rotated(HEADS)
         kv[chip, core, hf, :, HEAD:] = (
             acc[sl, (HEADS + 1) * HEAD :] + bv[...].astype(F32)
         ).astype(BF16)
-        kv_start(hf, (0, 1), (0, 3), (1, 0), (3, 0))
+        kv_start(hf, (0, 1), (0, 3), (1, 0), (3, 0), (0, 2))
         kv_sibling(0, hf).start()
         for h in range(HEADS):
             q = rotated(h)
             qn[h, sl, :] = q
             qt[:, pl.ds(h * ROWS + hf * HALF, HALF)] = q.T
 
-    issue(0)
-    issue(1)
+    for u in range(4):
+        issue(u)
     end0 = lengths[0]
     end1 = end0 + lengths[1]
     end2 = end1 + lengths[2]
@@ -226,7 +226,6 @@
         copy.wait()
     acc[...] = nn(tok[...], w[t])
     pump(0)
-    issue(2)
     for copy in loads_out:
         copy.wait()
     gacc[...] = nt(grad[...], wo[t])
@@ -234,22 +233,18 @@
     l_s[...] = jnp.zeros(l_s.shape, F32)
     oacc[...] = jnp.zeros(oacc.shape, F32)
     pump(1)
-    issue(3)
-    for hf in range(2):
-        sl = pl.ds(hf * HALF, HALF)
+    halves = [pl.ds(hf * HALF, HALF) for hf in range(2)]
+    for hf, sl in enumerate(halves):
         if hf == 1:
             pump(2)
-            issue(4)
             pump(3)
-            issue(5)
-        for u in (2 * hf, 2 * hf + 1):
-            rest(u)
+            for u in range(4, 7):
+                issue(u)
         acc[sl, :] += nn(tk[0, sl, :], w[left])
         acc[sl, :] += nn(tk[2, sl, :], w[right])
-        if hf == 1:
-            kv_second(0)
+    for hf, sl in enumerate(halves):
         for u in (2 * hf, 2 * hf + 1):
-            forward(u).wait_recv()
+            passed(u)
         acc[sl, :] += nn(tk[1, sl, :], w[opp])
         make_rows(hf)
 
@@ -287,6 +282,11 @@
                 m_s[:, sl] = top
                 held = (sl, weights.astype(BF16), shrink)
 
+    def gather_grad(hf):
+        sl = halves[hf]
+        gacc[sl, :] += nt(gr[0, sl, :], wo[left])
+        gacc[sl, :] += nt(gr[2, sl, :], wo[right])
+
     def forward_step(i, carry):
         j, hf = lax.rem(i + 3, 4), lax.div(i + 3, 4) - 1
         d = 2 * j + 1
@@ -294,20 +294,23 @@
 
         @pl.when(i == 1)
         def _():
+            pump(5)
+            gather_grad(0)
             kv_third(1)
-            pump(4)
-            kv_fourth(1)
             kv_fifth(0)
 
-        @pl.when(i == 3)
-        def _():
-            pump(5)
+        @pl.when(i == 2)
+        def _():
+            pump(6)
+
+        @pl.when(i == 4)
+        def _():
+            pump(7)
+
+        @pl.when(i == 5)
+        def _():
             kv_fifth(1)
-
-        @pl.when(i == 5)
-        def _():
-            pump(6)
-            pump(7)
+            gather_grad(1)
 
         for e in range(2):
             @pl.when((i > 0) & (chip >= d + e))
@@ -323,18 +326,14 @@
 
         return carry
 
-    issue(6)
     issue(7)
+    kv_second(0)
+    kv_second(1)
     kv_third(0)
-    kv_fourth(0)
-    kv_second(1)
+    pump(4)
     for hf in range(2):
         kv_sibling(0, hf).wait_recv()
     lax.fori_loop(0, REACH + 1, forward_step, 0)
-    for u in range(4, 8):
-        rest(u)
-    gacc[...] += nt(gr[0], wo[left])
-    gacc[...] += nt(gr[2], wo[right])
     for h in range(HEADS):
         sl = slice(h * ROWS, (h + 1) * ROWS)
         mass = l_s[:, sl]
@@ -365,28 +364,38 @@
         return remote(src, dst, rss.at[n, i], rsr.at[n, i], device)
 
     def scatter_early(share, part, arrived, passing, n):
-        for i, (slot, rel, e) in enumerate(((opp, 1, 0), (opp, 1, 1), (right, 2, 1), (left, 0, 0))):
-            sl = pl.ds(*pieces(n)[e])
-            part[rel, sl, :] = share(slot, sl).astype(BF16)
+        (first, rows), (second, _) = pieces(n)
+        both = pl.ds(first, 2 * rows)
+        part[1, both, :] = share(opp, both).astype(BF16)
+        for i in range(2):
             scatter_copy(i, part, arrived, passing, n).start()
-
-    def scatter_late(share, part, arrived, passing, n):
-        for i, (slot, rel, e) in enumerate(((right, 2, 0), (left, 0, 1))):
-            sl = pl.ds(*pieces(n)[e])
-            mine = share(slot, sl)
+        mine = share(right, both)
+        part[2, pl.ds(second, rows), :] = mine[rows:].astype(BF16)
+        scatter_copy(2, part, arrived, passing, n).start()
+        kept[0, pl.ds(0, rows), :] = mine[:rows]
+        mine = share(left, both)
+        part[0, pl.ds(first, rows), :] = mine[:rows].astype(BF16)
+        scatter_copy(3, part, arrived, passing, n).start()
+        kept[1, pl.ds(0, rows), :] = mine[rows:]
+
+    def scatter_late(part, arrived, passing, n):
+        for i, rel in ((0, 2), (1, 0)):
+            base, rows = pieces(n)[i]
             scatter_copy(i, part, arrived, passing, n).wait_recv()
-            part[rel, sl, :] = (mine + passing[i, passing_rows(n), :].astype(F32)).astype(BF16)
+            part[rel, pl.ds(base, rows), :] = (
+                kept[i, pl.ds(0, rows), :] + passing[i, passing_rows(n), :].astype(F32)
+            ).astype(BF16)
             scatter_copy(4 + i, part, arrived, passing, n).start()
 
     def scatter_end(share, part, arrived, passing, n, result):
-        for e, waits in ((1, (2, 5)), (0, (3, 4))):
-            sl = pl.ds(*pieces(n)[e])
-            mine = share(t, sl)
-            for i in waits:
-                scatter_copy(i, part, arrived, passing, n).wait_recv()
-            result[sl, :] = (
-                mine + arrived[0, sl, :].astype(F32) + arrived[1, sl, :].astype(F32)
-            ).astype(BF16)
+        (first, rows), _ = pieces(n)
+        both = pl.ds(first, 2 * rows)
+        mine = share(t, both)
+        for i in range(2, 6):
+            scatter_copy(i, part, arrived, passing, n).wait_recv()
+        result[both, :] = (
+            mine + arrived[0, both, :].astype(F32) + arrived[1, both, :].astype(F32)
+        ).astype(BF16)
         for i in range(6):
             scatter_copy(i, part, arrived, passing, n).wait_send()
 
@@ -398,7 +407,7 @@
     for hf in range(2):
         sl = pl.ds(hf * HALF, HALF)
         for u in (4 + 2 * hf, 5 + 2 * hf):
-            forward(u).wait_recv()
+            passed(u)
         g = (gacc[sl, :] + nt(gr[1, sl, :], wo[opp])).astype(BF16)
         for h in range(HEADS):
             part = g[:, h * HEAD : (h + 1) * HEAD]
@@ -471,7 +480,7 @@
 
         @pl.when(i == span - 1)
         def _():
-            scatter_late(out_share, p_out, v_out, f_out, 0)
+            scatter_late(p_out, v_out, f_out, 0)
 
         return carry
 
@@ -502,16 +511,16 @@
     finish_pair(0)
     scatter_early(grad_share, p_grad, v_grad, f_grad, 1)
     scatter_end(out_share, p_out, v_out, f_out, 0, out_ref)
-    scatter_late(grad_share, p_grad, v_grad, f_grad, 1)
+    scatter_late(p_grad, v_grad, f_grad, 1)
     finish_pair(1)
     scatter_early(grad_share, p_grad, v_grad, f_grad, 2)
     scatter_end(grad_share, p_grad, v_grad, f_grad, 1, gtok_ref)
-    scatter_late(grad_share, p_grad, v_grad, f_grad, 2)
+    scatter_late(p_grad, v_grad, f_grad, 2)
 
     for u in range(8):
         for way in range(2):
             send(u, way).wait_send()
-        forward(u).wait_send()
+            forward(u, way).wait_send()
     for hf in range(2):
         for j in range(1, 16):
             kv_copy(hf, j // 4, j % 4).wait_send()
@@ -523,6 +532,11 @@
                 if d > 0:
                     dkv_send(d, hf).wait_send()
     scatter_end(grad_share, p_grad, v_grad, f_grad, 2, gtok_ref)
+
+
+def hand_over(a, b, c, d):
+    c[...] = a[...]
+    d[...] = b[...]
 
 
 def local(
@@ -573,9 +587,10 @@
             pltpu.VMEM((3, ROWS, WIDTH), BF16),
             pltpu.VMEM((2, ROWS, WIDTH), BF16),
             pltpu.VMEM((2, HALF, WIDTH), BF16),
+            pltpu.VMEM((2, HALF, WIDTH), F32),
             dma((16,)),
             dma((8, 2)), dma((8, 2)),
-            dma((8,)), dma((8,)),
+            dma((8, 2)), dma((8, 2)),
             dma((2, 4, 4)), dma((2, 4, 4)),
             dma((REACH + 1, 2)), dma((REACH + 1, 2)),
             dma((REACH + 1, 2)), dma((REACH + 1, 2)),
@@ -588,9 +603,15 @@
         name="attention_block",
     )(
         doc_lengths, tokens, grad_out, w_query, w_key, value_weight, w_out,
-        b_query[None, :], key_bias[None, :], value_bias[None, :], freq,
+        b_query, key_bias, value_bias, freq,
     )
-    return results
+    return pl.pallas_call(
+        hand_over,
+        out_shape=(shape, shape),
+        in_specs=[vm, vm],
+        out_specs=(vm, vm),
+        name="hand_over",
+    )(*results)
 
 
 def solution(mesh):

time: 119 us -> 111 us (0.933)
  local copies, waits for them, and re-layouts: 5.19 us -> 0 us
  Pallas kernels: 113 us -> 110 us
    pallas_call x1, Pallas kernels: 113 us -> 108 us  [local(): pl.pallas_call(block_kernel, out_shape=(shape, shape), in_specs=[pl.Block...]
    unnamed x2 -> x0, local copies, waits for them, and re-layouts: 3.93 us -> none
    pallas_call x0 -> x1, Pallas kernels: none -> 2.38 us  [local(): pl.pallas_call(hand_over, out_shape=(shape, shape), in_specs=[vm, vm], ou...]
    broadcast_in_dim x1 -> x0, local copies, waits for them, and re-layouts: 1.26 us -> none  [local(): b_query[None, :]]
where the time goes in v4:
time: 111 us
  Pallas kernels  110 us (99%)
    pallas_call x1, Pallas kernels, local(): pl.pallas_call(block_kernel, out_shape=(shape, shape), in_specs=[pl.Block...  108 us
    pallas_call x1, Pallas kernels, local(): pl.pallas_call(hand_over, out_shape=(shape, shape), in_specs=[vm, vm], ou...  2.38 us

profile of v4, /device:TPU:64, one launch (start us, length us, event | category | flops | bytes accessed | tf_op | source)
XLA Modules:
  0.0 110.7 jit_solution(3776273677774948388)
XLA Ops:
  0.6 107.7 %attention_block.1 = (bf16[256,1280]{1,0:T(8,128)(2,1)}, bf16[256,1280]{1,0:T(8,128)(2,1)}) custom-call(s32[4]{0:T(128)} %lengths.1, bf16[256,1280]{1,0:T(8,128)(2,1)} %tok.1, bf16[256,1280]{1,0:T(8,128)(2,1)} %grad.1, bf16[5120,640]{1,0:T(8,128)(2,1)} %wq_hbm.1, bf16[5120,128]{1,0:T(8,128)(2,1)} %wk_hbm.1, bf16[5120,128]{1,0:T(8,128)(2,1)} %wv_hbm.1, ...), custom_call_target="tpu_custom_call" | custom-call | tf_op jit(solution)/shard_map/attention_block/pallas_call | solution.py:551
  108.3 2.4 %hand_over.1 = (bf16[256,1280]{1,0:T(8,128)(2,1)}, bf16[256,1280]{1,0:T(8,128)(2,1)}) custom-call(bf16[256,1280]{1,0:T(8,128)(2,1)} %get-tuple-element.4.a, bf16[256,1280]{1,0:T(8,128)(2,1)} %get-tuple-element.5.b), custom_call_target="tpu_custom_call" | custom-call | tf_op jit(solution)/shard_map/hand_over/pallas_call | solution.py:608

commit v5 on v4

--- a/solution.py
+++ b/solution.py
@@ -172,11 +172,22 @@
         kv_wait(hf, (3, 2))
         kv_start(hf, (2, 2))
 
-    def kv_fifth(hf):
-        kv_wait(hf, (1, 2), (1, 3), (3, 0), (3, 1), (2, 0), (2, 1), (2, 2), (2, 3))
-        for d in range(1, REACH + 1):
+    relayed = ((0, 1), (0, 2), (0, 3), (1, 0), (1, 1), (3, 2), (3, 3))
+
+    def kv_need(hf, *distances):
+        for d in distances:
             @pl.when(chip >= d)
             def _():
+                back_z = at_z - lax.div(chip - d, 4)
+                back_x = lax.rem(at_x + 4 - lax.rem(chip - d, 4), 4)
+                r1 = back_x + core * (back_z - back_x)
+                r2 = back_z + core * (back_x - back_z)
+                waited = (r2 == 0) | ((r2 == 1) & (r1 < 2)) | ((r2 == 3) & (r1 >= 2))
+
+                @pl.when(jnp.logical_not(waited))
+                def _():
+                    kv_wait(hf, (r2, r1))
+
                 kv_sibling(d, hf).start()
 
     def kv_sibling(d, hf):
@@ -253,7 +264,10 @@
 
     def attend(first, second):
         both = jnp.concatenate(
-            [kv[jnp.maximum(c, 0), :, hf].reshape(2 * HALF, 2 * HEAD) for c, hf in (first, second)],
+            [
+                kv[jnp.where(c < 0, chip, c), :, hf].reshape(2 * HALF, 2 * HEAD)
+                for c, hf in (first, second)
+            ],
             axis=0,
         )
         k = both[:, :HEAD]
@@ -287,50 +301,66 @@
         gacc[sl, :] += nt(gr[0, sl, :], wo[left])
         gacc[sl, :] += nt(gr[2, sl, :], wo[right])
 
+    near = ((4, 1), (3, 8), (5, 2), (7, 6))
+
+    def pick(j, e):
+        values = [pair[e] for pair in near]
+        return jnp.where(
+            j == 0, values[0], jnp.where(j == 1, values[1], jnp.where(j == 2, values[2], values[3]))
+        )
+
     def forward_step(i, carry):
         j, hf = lax.rem(i + 3, 4), lax.div(i + 3, 4) - 1
-        d = 2 * j + 1
         is_own = i == 0
+        ahead = (pick(j, 0), pick(j, 1))
 
         @pl.when(i == 1)
         def _():
+            kv_third(0)
+            kv_need(0, *near[0], *near[1])
+            kv_second(1)
+            pump(4)
+
+        @pl.when(i == 2)
+        def _():
             pump(5)
+
+        @pl.when(i == 3)
+        def _():
+            kv_need(0, *near[2])
             gather_grad(0)
+
+        @pl.when(i == 4)
+        def _():
+            kv_need(0, *near[3])
             kv_third(1)
-            kv_fifth(0)
-
-        @pl.when(i == 2)
-        def _():
+            kv_need(1, *near[0], *near[1])
             pump(6)
 
-        @pl.when(i == 4)
+        @pl.when(i == 5)
         def _():
             pump(7)
 
-        @pl.when(i == 5)
-        def _():
-            kv_fifth(1)
-            gather_grad(1)
-
-        for e in range(2):
-            @pl.when((i > 0) & (chip >= d + e))
+        @pl.when(i == 6)
+        def _():
+            kv_need(1, *near[2], *near[3])
+
+        for d in ahead:
+            @pl.when((i > 0) & (chip >= d))
             def _():
-                kv_sibling(d + e, hf).wait_recv()
-
-        @pl.when(is_own | (chip >= d))
+                kv_sibling(d, hf).wait_recv()
+
+        @pl.when(is_own | (chip >= jnp.minimum(*ahead)))
         def _():
             attend(
-                (jnp.where(is_own, chip, chip - d), jnp.where(is_own, 0, hf)),
-                (jnp.where(is_own, chip, chip - d - 1), jnp.where(is_own, 1, hf)),
+                (jnp.where(is_own, chip, chip - ahead[0]), jnp.where(is_own, 0, hf)),
+                (jnp.where(is_own, chip, chip - ahead[1]), jnp.where(is_own, 1, hf)),
             )
 
         return carry
 
     issue(7)
     kv_second(0)
-    kv_second(1)
-    kv_third(0)
-    pump(4)
     for hf in range(2):
         kv_sibling(0, hf).wait_recv()
     lax.fori_loop(0, REACH + 1, forward_step, 0)
@@ -404,6 +434,7 @@
 
     scatter_early(out_share, p_out, v_out, f_out, 0)
 
+    gather_grad(1)
     for hf in range(2):
         sl = pl.ds(hf * HALF, HALF)
         for u in (4 + 2 * hf, 5 + 2 * hf):
@@ -523,7 +554,14 @@
             forward(u, way).wait_send()
     for hf in range(2):
         for j in range(1, 16):
-            kv_copy(hf, j // 4, j % 4).wait_send()
+            slot = (j // 4, j % 4)
+            kv_copy(hf, *slot).wait_send()
+            if slot not in relayed:
+                gap = chip - place(*slot)
+
+                @pl.when((gap < 1) | (gap > REACH))
+                def _():
+                    kv_wait(hf, slot)
         for d in range(REACH + 1):
             @pl.when(chip >= d)
             def _():

time: 111 us -> 109 us (0.982)
    pallas_call x1, Pallas kernels: 108 us -> 106 us  [local(): pl.pallas_call(block_kernel, out_shape=(shape, shape), in_specs=[pl.Block...]
where the time goes in v5:
time: 109 us
  Pallas kernels  109 us (100%)
    pallas_call x1, Pallas kernels, local(): pl.pallas_call(block_kernel, out_shape=(shape, shape), in_specs=[pl.Block...  106 us
    pallas_call x1, Pallas kernels, local(): pl.pallas_call(hand_over, out_shape=(shape, shape), in_specs=[vm, vm], ou...  2.38 us

profile of v5, /device:TPU:64, one launch (start us, length us, event | category | flops | bytes accessed | tf_op | source)
XLA Modules:
  0.0 109.2 jit_solution(1695801966225179175)
XLA Ops:
  0.6 106.2 %attention_block.1 = (bf16[256,1280]{1,0:T(8,128)(2,1)}, bf16[256,1280]{1,0:T(8,128)(2,1)}) custom-call(s32[4]{0:T(128)} %lengths.1, bf16[256,1280]{1,0:T(8,128)(2,1)} %tok.1, bf16[256,1280]{1,0:T(8,128)(2,1)} %grad.1, bf16[5120,640]{1,0:T(8,128)(2,1)} %wq_hbm.1, bf16[5120,128]{1,0:T(8,128)(2,1)} %wk_hbm.1, bf16[5120,128]{1,0:T(8,128)(2,1)} %wv_hbm.1, ...), custom_call_target="tpu_custom_call" | custom-call | tf_op jit(solution)/shard_map/attention_block/pallas_call | solution.py:589
  106.8 2.4 %hand_over.1 = (bf16[256,1280]{1,0:T(8,128)(2,1)}, bf16[256,1280]{1,0:T(8,128)(2,1)}) custom-call(bf16[256,1280]{1,0:T(8,128)(2,1)} %get-tuple-element.4.a, bf16[256,1280]{1,0:T(8,128)(2,1)} %get-tuple-element.5.b), custom_call_target="tpu_custom_call" | custom-call | tf_op jit(solution)/shard_map/hand_over/pallas_call | solution.py:646

commit v6 on v5

--- a/solution.py
+++ b/solution.py
@@ -296,11 +296,6 @@
                 m_s[:, sl] = top
                 held = (sl, weights.astype(BF16), shrink)
 
-    def gather_grad(hf):
-        sl = halves[hf]
-        gacc[sl, :] += nt(gr[0, sl, :], wo[left])
-        gacc[sl, :] += nt(gr[2, sl, :], wo[right])
-
     near = ((4, 1), (3, 8), (5, 2), (7, 6))
 
     def pick(j, e):
@@ -327,12 +322,10 @@
 
         @pl.when(i == 3)
         def _():
-            kv_need(0, *near[2])
-            gather_grad(0)
+            kv_need(0, *near[2], *near[3])
 
         @pl.when(i == 4)
         def _():
-            kv_need(0, *near[3])
             kv_third(1)
             kv_need(1, *near[0], *near[1])
             pump(6)
@@ -434,16 +427,15 @@
 
     scatter_early(out_share, p_out, v_out, f_out, 0)
 
-    gather_grad(1)
-    for hf in range(2):
-        sl = pl.ds(hf * HALF, HALF)
-        for u in (4 + 2 * hf, 5 + 2 * hf):
-            passed(u)
-        g = (gacc[sl, :] + nt(gr[1, sl, :], wo[opp])).astype(BF16)
-        for h in range(HEADS):
-            part = g[:, h * HEAD : (h + 1) * HEAD]
-            gn[h, sl, :] = part
-            gt[:, pl.ds(h * ROWS + hf * HALF, HALF)] = part.T
+    for u in range(4, 8):
+        passed(u)
+    g = gacc[...] + nt(gr[0], wo[left])
+    g = g + nt(gr[2], wo[right])
+    g = (g + nt(gr[1], wo[opp])).astype(BF16)
+    for h in range(HEADS):
+        part = g[:, h * HEAD : (h + 1) * HEAD]
+        gn[h] = part
+        gt[:, h * ROWS : (h + 1) * ROWS] = part.T
     delta[...] = jnp.sum(gt[...].astype(F32) * att[...].astype(F32), axis=0, keepdims=True)
     oacc[...] = jnp.zeros(oacc.shape, F32)
 
@@ -509,18 +501,21 @@
         def _():
             dkv_pump(i - 1)
 
-        @pl.when(i == span - 1)
+        @pl.when(i == span - 2)
         def _():
             scatter_late(p_out, v_out, f_out, 0)
 
         return carry
 
     lax.fori_loop(0, 2 * span, backward_step, 0)
-    for h in range(HEADS):
-        u = oacc[:, h * ROWS : (h + 1) * ROWS].T * factor
-        x[:, h * HEAD : (h + 1) * HEAD] = (
-            u * cos_ref[...] - pltpu.roll(u, HEAD // 2, 1) * sin_ref[...]
-        ).astype(BF16)
+    def query_rows(hf):
+        sl = halves[hf]
+        for h in range(HEADS):
+            u = oacc[:, pl.ds(h * ROWS + hf * HALF, HALF)].T * factor
+            x[sl, h * HEAD : (h + 1) * HEAD] = (
+                u * cos_ref[sl, :] - pltpu.roll(u, HEAD // 2, 1) * sin_ref[sl, :]
+            ).astype(BF16)
+
     def finish_pair(hf):
         dkv_sibling(0, hf).wait_recv()
         own[0, hf] = own[0, hf] + sib_in[0, hf].astype(F32)
@@ -539,8 +534,10 @@
     def grad_share(slot, sl):
         return nt(x[sl, :], w[slot])
 
+    query_rows(0)
     finish_pair(0)
     scatter_early(grad_share, p_grad, v_grad, f_grad, 1)
+    query_rows(1)
     scatter_end(out_share, p_out, v_out, f_out, 0, out_ref)
     scatter_late(p_grad, v_grad, f_grad, 1)
     finish_pair(1)

time: 109 us -> 109 us (level)
  no operation moved by 1% of the time
where the time goes in v6:
time: 109 us
  Pallas kernels  108 us (99%)
    pallas_call x1, Pallas kernels, local(): pl.pallas_call(block_kernel, out_shape=(shape, shape), in_specs=[pl.Block...  106 us
    pallas_call x1, Pallas kernels, local(): pl.pallas_call(hand_over, out_shape=(shape, shape), in_specs=[vm, vm], ou...  2.38 us

profile of v6, /device:TPU:64, one launch (start us, length us, event | category | flops | bytes accessed | tf_op | source)
XLA Modules:
  0.0 108.8 jit_solution(7535123886639297816)
XLA Ops:
  0.6 105.8 %attention_block.1 = (bf16[256,1280]{1,0:T(8,128)(2,1)}, bf16[256,1280]{1,0:T(8,128)(2,1)}) custom-call(s32[4]{0:T(128)} %lengths.1, bf16[256,1280]{1,0:T(8,128)(2,1)} %tok.1, bf16[256,1280]{1,0:T(8,128)(2,1)} %grad.1, bf16[5120,640]{1,0:T(8,128)(2,1)} %wq_hbm.1, bf16[5120,128]{1,0:T(8,128)(2,1)} %wk_hbm.1, bf16[5120,128]{1,0:T(8,128)(2,1)} %wv_hbm.1, ...), custom_call_target="tpu_custom_call" | custom-call | tf_op jit(solution)/shard_map/attention_block/pallas_call | solution.py:586
  106.4 2.4 %hand_over.1 = (bf16[256,1280]{1,0:T(8,128)(2,1)}, bf16[256,1280]{1,0:T(8,128)(2,1)}) custom-call(bf16[256,1280]{1,0:T(8,128)(2,1)} %get-tuple-element.4.a, bf16[256,1280]{1,0:T(8,128)(2,1)} %get-tuple-element.5.b), custom_call_target="tpu_custom_call" | custom-call | tf_op jit(solution)/shard_map/hand_over/pallas_call | solution.py:643

commit v7 on v6

--- a/solution.py
+++ b/solution.py
@@ -569,9 +569,23 @@
     scatter_end(grad_share, p_grad, v_grad, f_grad, 2, gtok_ref)
 
 
-def hand_over(a, b, c, d):
-    c[...] = a[...]
-    d[...] = b[...]
+def hand_over(a, b, c, d, held, came, left):
+    chunks = [
+        (i, j, pl.ds(j * CHUNK, CHUNK)) for j in range(ROWS // CHUNK) for i in range(2)
+    ]
+    arrive = [
+        pltpu.make_async_copy((a, b)[i].at[sl], held.at[i, sl], came.at[i, j]) for i, j, sl in chunks
+    ]
+    depart = [
+        pltpu.make_async_copy(held.at[i, sl], (c, d)[i].at[sl], left.at[i, j]) for i, j, sl in chunks
+    ]
+    for copy in arrive:
+        copy.start()
+    for before, after in zip(arrive, depart):
+        before.wait()
+        after.start()
+    for copy in depart:
+        copy.wait()
 
 
 def local(
@@ -643,8 +657,13 @@
     return pl.pallas_call(
         hand_over,
         out_shape=(shape, shape),
-        in_specs=[vm, vm],
-        out_specs=(vm, vm),
+        in_specs=[hbm, hbm],
+        out_specs=(hbm, hbm),
+        scratch_shapes=[
+            pltpu.VMEM((2, ROWS, WIDTH), BF16),
+            dma((2, ROWS // CHUNK)),
+            dma((2, ROWS // CHUNK)),
+        ],
         name="hand_over",
     )(*results)
 

time: 109 us -> 109 us (level)
  no operation moved by 1% of the time
where the time goes in v7:
time: 109 us
  Pallas kernels  108 us (99%)
    pallas_call x1, Pallas kernels, local(): pl.pallas_call(block_kernel, out_shape=(shape, shape), in_specs=[pl.Block...  106 us
    pallas_call x1, Pallas kernels, local(): pl.pallas_call(hand_over, out_shape=(shape, shape), in_specs=[hbm, hbm],...  2.21 us

profile of v7, /device:TPU:64, one launch (start us, length us, event | category | flops | bytes accessed | tf_op | source)
XLA Modules:
  0.0 108.8 jit_solution(1193091050486807822)
XLA Ops:
  0.6 105.8 %attention_block.1 = (bf16[256,1280]{1,0:T(8,128)(2,1)}, bf16[256,1280]{1,0:T(8,128)(2,1)}) custom-call(s32[4]{0:T(128)} %lengths.1, bf16[256,1280]{1,0:T(8,128)(2,1)} %tok.1, bf16[256,1280]{1,0:T(8,128)(2,1)} %grad.1, bf16[5120,640]{1,0:T(8,128)(2,1)} %wq_hbm.1, bf16[5120,128]{1,0:T(8,128)(2,1)} %wk_hbm.1, bf16[5120,128]{1,0:T(8,128)(2,1)} %wv_hbm.1, ...), custom_call_target="tpu_custom_call" | custom-call | tf_op jit(solution)/shard_map/attention_block/pallas_call | solution.py:600
  106.4 2.2 %hand_over.1 = (bf16[256,1280]{1,0:T(8,128)(2,1)}, bf16[256,1280]{1,0:T(8,128)(2,1)}) custom-call(bf16[256,1280]{1,0:T(8,128)(2,1)} %get-tuple-element.4.a, bf16[256,1280]{1,0:T(8,128)(2,1)} %get-tuple-element.5.b), custom_call_target="tpu_custom_call" | custom-call | tf_op jit(solution)/shard_map/hand_over/pallas_call | solution.py:657
